TPU v7x, 32 devices: a whole 2x2x4 slice. The times are simulated.
32 devices in a mesh: row: 4 (over y, core), col: 8 (over z, x).
Axes of the slice: x: 2, y: 2, z: 4, core: 2. Of those that a mesh axis runs over, the one named last changes fastest.
Arguments:
- raster: bfloat16 [64, 128, 1024], P(None, 'row', 'col')
- conv_one: bfloat16 [64, 576], replicated, may hold values from -0.25 to 0.25
- bias_one: float32 [64], replicated, may hold values from -3 to 3
- conv_two: bfloat16 [64, 576], replicated, may hold values from -0.25 to 0.25
- bias_two: float32 [64], replicated, may hold values from -3 to 3
- pos_embed: bfloat16 [64, 4, 32], P(None, 'row', 'col'), may hold values from -6 to 6
- query_embed: bfloat16 [256, 256], replicated
- w_query: bfloat16 [256, 256], replicated, may hold values from -0.375 to 0.375
- w_key: bfloat16 [64, 256], replicated, may hold values from -0.75 to 0.75
- w_value: bfloat16 [64, 256], replicated, may hold values from -0.75 to 0.75
- w_out: bfloat16 [256, 256], replicated, may hold values from -0.375 to 0.375
- visible: int32 [2, 32], replicated, may hold values from 0 to 1, as said below
Outputs:
- map_queries: bfloat16 [256, 256], P(('row', 'col'))
Inputs may be any that keep to these rules, and one draw needn't show every extreme that they name: `visible`: every query block sees at least one tile; each block sees a square of tiles around one tile and, independently, about one in eight of the other tiles.
All inputs are finite; a program needn't handle non-finite values.
Results may differ from a plain program's by a relative error of at most 0.035.
Values may be sent and summed in bfloat16 or wider, within the bound.
A program may use at most 128 MiB of HBM per device.

v0:
```python
import jax
import jax.numpy as jnp
from jax import lax
from jax.sharding import PartitionSpec as P

E = 256
HEADS = 8
HEAD_DIM = 32
PATCH = 32
QBLOCK = 128


def padded_2(shard, sides, width):
    for axis, dim in sides:
        peers, length = (lax.axis_size(axis), shard.shape[dim])
        up = [(i, (i + 1) % peers) for i in range(peers - 1)]
        down = [(j, i) for i, j in up]
        last = lax.slice_in_dim(shard, length - width, length, axis=dim)
        leading = lax.slice_in_dim(shard, 0, width, axis=dim)
        before = lax.ppermute(last, axis, up)
        after = lax.ppermute(leading, axis, down)
        shard = jnp.concatenate([before, shard, after], axis=dim)
    return shard


def conv_layer(padded, weight, bias):
    out_rows = padded.shape[1] - 2
    width = padded.shape[2] - 2
    count = min(32, out_rows)
    taps = [padded[:, dy : dy + count, dx : dx + width] for dy in range(3) for dx in range(3)]
    stacked = jnp.concatenate(taps, 0)
    out = jnp.einsum("ok,khw->ohw", weight, stacked, preferred_element_type=jnp.float32)
    pieces = jnp.maximum(out + bias[:, None, None], 0.0)
    return pieces


def finish(total, mixed, w_out):
    count = mixed.shape[0]
    attended = (
        (mixed.reshape(count, HEADS, HEAD_DIM) / total[..., None])
        .reshape(count, E)
        .astype(jnp.bfloat16)
    )
    return jnp.dot(attended, w_out, preferred_element_type=jnp.float32).astype(jnp.bfloat16)


def fold_step(carry, key_piece, value_piece, query_heads, seen_row, local_count, scale):
    peak_old, total_old, mixed_old = carry
    owned = query_heads.shape[0]
    tile_count = seen_row.shape[0]
    count = key_piece.shape[0]
    tiles = jnp.arange(count, dtype=jnp.int32) // local_count
    match = tiles[:, None] == jnp.arange(tile_count, dtype=jnp.int32)[None, :]
    seen = jnp.sum(jnp.where(match, seen_row[None, :], 0), axis=1) > 0
    score = (
        jnp.einsum(
            "qhd,khd->qhk",
            query_heads,
            key_piece.reshape(count, HEADS, HEAD_DIM),
            preferred_element_type=jnp.float32,
        )
        * scale
    )
    score = jnp.where(seen[None, None, :], score, -1e30)
    top = jnp.maximum(peak_old, jnp.max(score, axis=-1))
    weight = jnp.where(seen[None, None, :], jnp.exp(score - top[..., None]), 0.0)
    mixed_new = jnp.einsum(
        "qhk,khd->qhd",
        weight.astype(jnp.bfloat16),
        value_piece.reshape(count, HEADS, HEAD_DIM),
        preferred_element_type=jnp.float32,
    )
    return (top, jnp.sum(weight, axis=-1), mixed_new.reshape(owned, E))


def on_device(
    raster,
    conv_one,
    bias_one,
    conv_two,
    bias_two,
    pos_embed,
    query_embed,
    w_query,
    w_key,
    w_value,
    w_out,
    visible,
):
    rows = raster.shape[1]
    cols = raster.shape[2]

    def widen(field):
        return padded_2(field, (("row", 1), ("col", 2)), 1)

    first = conv_layer(widen(raster), conv_one, bias_one).astype(jnp.bfloat16)
    second = conv_layer(widen(first), conv_two, bias_two)
    channels = second.shape[0]
    pooled = second.reshape(channels, rows // PATCH, PATCH, cols // PATCH, PATCH).mean(axis=(2, 4))
    tokens = (pooled + pos_embed.astype(jnp.float32)).astype(jnp.bfloat16)
    local_count = rows // PATCH * (cols // PATCH)
    flat = tokens.reshape(channels, local_count).T
    scale = 1.0 / HEAD_DIM**0.5
    all_queries = query_embed.shape[0]
    devices = lax.axis_size("row") * lax.axis_size("col")
    owned = all_queries // devices
    owner = lax.axis_index("row") * lax.axis_size("col") + lax.axis_index("col")
    start_state = (
        jnp.full((owned, HEADS), -1e30, jnp.float32),
        jnp.zeros((owned, HEADS), jnp.float32),
        jnp.zeros((owned, E), jnp.float32),
    )
    own_embed = lax.dynamic_slice_in_dim(query_embed, owner * owned, owned, 0)
    own_queries = jnp.dot(own_embed, w_query, preferred_element_type=jnp.float32).astype(
        jnp.bfloat16
    )
    query_heads = own_queries.reshape(owned, HEADS, HEAD_DIM)
    seen_row = lax.dynamic_slice_in_dim(visible, owner * owned // QBLOCK, 1, 0)[0]
    piece = lax.all_gather(flat, ("row", "col"), axis=0, tiled=True)
    key_piece = jnp.dot(piece, w_key, preferred_element_type=jnp.float32).astype(jnp.bfloat16)
    value_piece = jnp.dot(piece, w_value, preferred_element_type=jnp.float32).astype(jnp.bfloat16)
    peak, total, mixed = fold_step(
        start_state, key_piece, value_piece, query_heads, seen_row, local_count, scale
    )
    return finish(total, mixed, w_out)


def solution(mesh):
    in_specs = (
        P(None, "row", "col"),
        P(),
        P(),
        P(),
        P(),
        P(None, "row", "col"),
        P(),
        P(),
        P(),
        P(),
        P(),
        P(),
    )
    out_specs = P(("row", "col"), None)
    return jax.shard_map(
        on_device, mesh=mesh, in_specs=in_specs, out_specs=out_specs, check_vma=False
    )
```

profile of v0, /device:TPU:0, one launch (start us, length us, event | category | flops | bytes accessed | tf_op | source)
XLA Modules:
  0.0 120.1 jit_solution(11906341822449594353)
XLA Ops:
  0.0 1.3 %copy.69 = bf16[64,32,128]{2,0,1:T(8,128)(2,1)S(1)} copy(bf16[64,32,128]{2,1,0:T(8,128)(2,1)} %param.12) | data formatting | bytes 1048576 | tf_op args[0]
  1.3 2.4 %collective-permute-start = (bf16[64,1,128]{2,0,1:T(8,128)(2,1)S(1)}, bf16[64,1,128]{2,0,1:T(8,128)(2,1)S(1)}, u32[]{:S(2)}, u32[]{:S(2)}) collective-permute-start(bf16[64,1,128]{2,0,1:T(8,128)(2,1)S(1)} %get-tuple-element.14), channel_id=1, source_target_pairs={{0,8},{8,16},{16,24},{1,9},{9,17},{17,25},{2,10},{10,18},{18,26},{... | collective-permute-start | bytes 49160 | tf_op jit(solution)/shard_map/ppermute | solution.py:20
  3.7 1.3 %collective-permute-start.1 = (bf16[64,1,128]{2,0,1:T(8,128)(2,1)S(1)}, bf16[64,1,128]{2,0,1:T(8,128)(2,1)S(1)}, u32[]{:S(2)}, u32[]{:S(2)}) collective-permute-start(bf16[64,1,128]{2,0,1:T(8,128)(2,1)S(1)} %get-tuple-element.13), channel_id=1, source_target_pairs={{8,0},{16,8},{24,16},{9,1},{17,9},{25,17},{10,2},{18,10},{26,18},{... | collective-permute-start | bytes 49160 | tf_op jit(solution)/shard_map/ppermute | solution.py:21
  5.8 1.3 %constant_dynamic-update-slice_fusion.1 = bf16[64,34,128]{2,0,1:T(8,128)(2,1)S(1)} fusion(bf16[64,34,128]{2,0,1:T(8,128)(2,1)S(1)} %constant_dynamic-update-slice_fusion.2, bf16[64,32,128]{2,1,0:T(8,128)(2,1)} %param.12), kind=kLoop, calls=%fused_computation.58 | loop fusion | bytes 1048576
  7.1 1.8 %collective-permute-done.1 = bf16[64,1,128]{2,0,1:T(8,128)(2,1)S(1)} collective-permute-done((bf16[64,1,128]{2,0,1:T(8,128)(2,1)S(1)}, bf16[64,1,128]{2,0,1:T(8,128)(2,1)S(1)}, u32[]{:S(2)}, u32[]{:S(2)}) %collective-permute-start.1) | collective-permute-done | bytes 16416 | tf_op jit(solution)/shard_map/ppermute | solution.py:21
  9.5 3.4 %collective-permute-start.2 = (bf16[64,34,1]{0,1,2:T(8,128)(2,1)S(1)}, bf16[64,34,1]{0,1,2:T(8,128)(2,1)S(1)}, u32[]{:S(2)}, u32[]{:S(2)}) collective-permute-start(bf16[64,34,1]{0,1,2:T(8,128)(2,1)S(1)} %copy.72), channel_id=1, source_target_pairs={{0,1},{1,2},{2,3},{3,4},{4,5},{5,6},{6,7},{8,9},{9,10},{10,11},{11... | collective-permute-start | bytes 13064 | tf_op jit(solution)/shard_map/ppermute | solution.py:20
  13.2 1.3 %collective-permute-start.3 = (bf16[64,34,1]{0,1,2:T(8,128)(2,1)S(1)}, bf16[64,34,1]{0,1,2:T(8,128)(2,1)S(1)}, u32[]{:S(2)}, u32[]{:S(2)}) collective-permute-start(bf16[64,34,1]{0,1,2:T(8,128)(2,1)S(1)} %copy.75), channel_id=1, source_target_pairs={{1,0},{2,1},{3,2},{4,3},{5,4},{6,5},{7,6},{9,8},{10,9},{11,10},{12... | collective-permute-start | bytes 13064 | tf_op jit(solution)/shard_map/ppermute | solution.py:21
  14.9 1.1 fusion.16
  16.9 1.9 %collective-permute-done.3 = bf16[64,34,1]{0,1,2:T(8,128)(2,1)S(1)} collective-permute-done((bf16[64,34,1]{0,1,2:T(8,128)(2,1)S(1)}, bf16[64,34,1]{0,1,2:T(8,128)(2,1)S(1)}, u32[]{:S(2)}, u32[]{:S(2)}) %collective-permute-start.3) | collective-permute-done | bytes 4384 | tf_op jit(solution)/shard_map/ppermute | solution.py:21
  19.2 1.2 %fusion.12 = bf16[576,32,128]{2,0,1:T(8,128)(2,1)} fusion(bf16[576,32,128]{2,0,1:T(8,128)(2,1)} %fusion.22, bf16[64,34,128]{2,0,1:T(8,128)(2,1)S(1)} %constant_dynamic-update-slice_fusion, bf16[64,34,1]{2,0,1:T(8,128)(2,1)S(1)} %copy.76), kind=kLoop, calls=%fused_computation.31 | loop fusion | flops 1048576 | bytes 1085696
  20.4 1.1 fusion.14
  21.5 1.0 constant_dynamic-update-slice_fusion.3
  22.5 1.2 %fusion.10 = bf16[576,32,128]{2,0,1:T(8,128)(2,1)} fusion(bf16[576,32,128]{2,0,1:T(8,128)(2,1)} %constant_dynamic-update-slice_fusion.3, bf16[64,34,128]{2,0,1:T(8,128)(2,1)S(1)} %constant_dynamic-update-slice_fusion, bf16[64,34,1]{2,0,1:T(8,128)(2,1)S(1)} %copy.76), kind=kLoop, calls=%fused_computation.29 | loop fusion | flops 1048576 | bytes 1085696
  23.7 1.1 fusion.21
  25.8 1.2 %fusion.19 = bf16[576,32,128]{2,0,1:T(8,128)(2,1)} fusion(bf16[576,32,128]{2,0,1:T(8,128)(2,1)} %fusion.20, bf16[64,34,1]{2,0,1:T(8,128)(2,1)S(1)} %copy.76, bf16[64,34,128]{2,0,1:T(8,128)(2,1)S(1)} %constant_dynamic-update-slice_fusion), kind=kLoop, calls=%fused_computation.47 | loop fusion | flops 1048576 | bytes 1085696 | tf_op jit(solution)/shard_map/concatenate | solution.py:31
  27.0 3.4 %fusion.4 = bf16[64,32,128]{2,0,1:T(8,128)(2,1)S(1)} fusion(bf16[576,32,128]{2,0,1:T(8,128)(2,1)} %fusion.19, f32[64]{0:T(128)S(1)} %copy-done.8, bf16[64,576]{1,0:T(8,128)(2,1)S(1)} %copy-done.3), kind=kOutput, calls=%fused_computation.14 | convolution fusion | flops 302776320 | bytes 5316864 | tf_op jit(solution)/shard_map/ok,khw->ohw/dot_general | solution.py:32
  30.4 3.0 %collective-permute-start.4 = (bf16[64,1,128]{2,0,1:T(8,128)(2,1)S(1)}, bf16[64,1,128]{2,0,1:T(8,128)(2,1)S(1)}, u32[]{:S(2)}, u32[]{:S(2)}) collective-permute-start(bf16[64,1,128]{2,0,1:T(8,128)(2,1)S(1)} %get-tuple-element.11), channel_id=1, source_target_pairs={{0,8},{8,16},{16,24},{1,9},{9,17},{17,25},{2,10},{10,18},{18,26},{... | collective-permute-start | bytes 49160 | tf_op jit(solution)/shard_map/ppermute | solution.py:20
  33.4 1.3 %collective-permute-start.5 = (bf16[64,1,128]{2,0,1:T(8,128)(2,1)S(1)}, bf16[64,1,128]{2,0,1:T(8,128)(2,1)S(1)}, u32[]{:S(2)}, u32[]{:S(2)}) collective-permute-start(bf16[64,1,128]{2,0,1:T(8,128)(2,1)S(1)} %get-tuple-element.12), channel_id=1, source_target_pairs={{8,0},{16,8},{24,16},{9,1},{17,9},{25,17},{10,2},{18,10},{26,18},{... | collective-permute-start | bytes 49160 | tf_op jit(solution)/shard_map/ppermute | solution.py:21
  34.8 3.4 %collective-permute-done.5 = bf16[64,1,128]{2,0,1:T(8,128)(2,1)S(1)} collective-permute-done((bf16[64,1,128]{2,0,1:T(8,128)(2,1)S(1)}, bf16[64,1,128]{2,0,1:T(8,128)(2,1)S(1)}, u32[]{:S(2)}, u32[]{:S(2)}) %collective-permute-start.5) | collective-permute-done | bytes 16416 | tf_op jit(solution)/shard_map/ppermute | solution.py:21
  38.8 4.3 %collective-permute-start.6 = (bf16[64,34,1]{0,1,2:T(8,128)(2,1)S(1)}, bf16[64,34,1]{0,1,2:T(8,128)(2,1)S(1)}, u32[]{:S(2)}, u32[]{:S(2)}) collective-permute-start(bf16[64,34,1]{0,1,2:T(8,128)(2,1)S(1)} %copy.79), channel_id=1, source_target_pairs={{0,1},{1,2},{2,3},{3,4},{4,5},{5,6},{6,7},{8,9},{9,10},{10,11},{11... | collective-permute-start | bytes 13064 | tf_op jit(solution)/shard_map/ppermute | solution.py:20
  43.5 1.3 %collective-permute-start.7 = (bf16[64,34,1]{0,1,2:T(8,128)(2,1)S(1)}, bf16[64,34,1]{0,1,2:T(8,128)(2,1)S(1)}, u32[]{:S(2)}, u32[]{:S(2)}) collective-permute-start(bf16[64,34,1]{0,1,2:T(8,128)(2,1)S(1)} %copy.81), channel_id=1, source_target_pairs={{1,0},{2,1},{3,2},{4,3},{5,4},{6,5},{7,6},{9,8},{10,9},{11,10},{12... | collective-permute-start | bytes 13064 | tf_op jit(solution)/shard_map/ppermute | solution.py:21
  45.3 3.8 %collective-permute-done.7 = bf16[64,34,1]{0,1,2:T(8,128)(2,1)S(1)} collective-permute-done((bf16[64,34,1]{0,1,2:T(8,128)(2,1)S(1)}, bf16[64,34,1]{0,1,2:T(8,128)(2,1)S(1)}, u32[]{:S(2)}, u32[]{:S(2)}) %collective-permute-start.7) | collective-permute-done | bytes 4384 | tf_op jit(solution)/shard_map/ppermute | solution.py:21
  51.9 1.0 fusion.3
  53.1 65.0 %all-gather = bf16[32,4,64]{2,1,0:T(4,128)(2,1)S(1)} all-gather(bf16[1,4,64]{2,1,0:T(4,128)(2,1)S(1)} %fusion.34), channel_id=1, replica_groups=mesh['row'=4,'col'=8] {'row','col'}, dimensions={0}, use_global_device_ids=true | all-gather | bytes 16896 | tf_op jit(solution)/shard_map/all_gather | solution.py:119
  (73 shorter events, 10.7 us)
Async XLA Ops:
  0.0 5.0 %copy-start = (bf16[256,256]{1,0:T(8,128)(2,1)S(1)}, bf16[256,256]{1,0:T(8,128)(2,1)}, u32[]{:S(2)}) copy-start(bf16[256,256]{1,0:T(8,128)(2,1)} %param.19) | copy-start | bytes 393220
  0.0 12.9 %copy-start.10 = (s32[2,32]{1,0:T(2,128)S(1)}, s32[2,32]{1,0:T(2,128)}, u32[]{:S(2)}) copy-start(s32[2,32]{1,0:T(2,128)} %param.23) | copy-start | bytes 772
  1.3 4.5 %collective-permute-start = (bf16[64,1,128]{2,0,1:T(8,128)(2,1)S(1)}, bf16[64,1,128]{2,0,1:T(8,128)(2,1)S(1)}, u32[]{:S(2)}, u32[]{:S(2)}) collective-permute-start(bf16[64,1,128]{2,0,1:T(8,128)(2,1)S(1)} %get-tuple-element.14), channel_id=1, source_target_pairs={{0,8},{8,16},{16,24},{1,9},{9,17},{17,25},{2,10},{10,18},{18,26},{... | collective-permute-start | bytes 49160 | tf_op jit(solution)/shard_map/ppermute | solution.py:20
  3.7 5.2 %collective-permute-start.1 = (bf16[64,1,128]{2,0,1:T(8,128)(2,1)S(1)}, bf16[64,1,128]{2,0,1:T(8,128)(2,1)S(1)}, u32[]{:S(2)}, u32[]{:S(2)}) collective-permute-start(bf16[64,1,128]{2,0,1:T(8,128)(2,1)S(1)} %get-tuple-element.13), channel_id=1, source_target_pairs={{8,0},{16,8},{24,16},{9,1},{17,9},{25,17},{10,2},{18,10},{26,18},{... | collective-permute-start | bytes 49160 | tf_op jit(solution)/shard_map/ppermute | solution.py:21
  8.9 12.6 %copy-start.1 = (bf16[64,32,128]{2,1,0:T(8,128)(2,1)S(1)}, bf16[64,32,128]{2,1,0:T(8,128)(2,1)}, u32[]{:S(2)}) copy-start(bf16[64,32,128]{2,1,0:T(8,128)(2,1)} %param.12) | copy-start | bytes 1572868
  9.5 5.0 %collective-permute-start.2 = (bf16[64,34,1]{0,1,2:T(8,128)(2,1)S(1)}, bf16[64,34,1]{0,1,2:T(8,128)(2,1)S(1)}, u32[]{:S(2)}, u32[]{:S(2)}) collective-permute-start(bf16[64,34,1]{0,1,2:T(8,128)(2,1)S(1)} %copy.72), channel_id=1, source_target_pairs={{0,1},{1,2},{2,3},{3,4},{4,5},{5,6},{6,7},{8,9},{9,10},{10,11},{11... | collective-permute-start | bytes 13064 | tf_op jit(solution)/shard_map/ppermute | solution.py:20
  13.2 5.6 %collective-permute-start.3 = (bf16[64,34,1]{0,1,2:T(8,128)(2,1)S(1)}, bf16[64,34,1]{0,1,2:T(8,128)(2,1)S(1)}, u32[]{:S(2)}, u32[]{:S(2)}) collective-permute-start(bf16[64,34,1]{0,1,2:T(8,128)(2,1)S(1)} %copy.75), channel_id=1, source_target_pairs={{1,0},{2,1},{3,2},{4,3},{5,4},{6,5},{7,6},{9,8},{10,9},{11,10},{12... | collective-permute-start | bytes 13064 | tf_op jit(solution)/shard_map/ppermute | solution.py:21
  20.4 6.6 %copy-start.3 = (bf16[64,576]{1,0:T(8,128)(2,1)S(1)}, bf16[64,576]{1,0:T(8,128)(2,1)}, u32[]{:S(2)}) copy-start(bf16[64,576]{1,0:T(8,128)(2,1)} %param.13) | copy-start | bytes 221188
  20.4 6.7 %copy-start.8 = (f32[64]{0:T(128)S(1)}, f32[64]{0:T(128)}, u32[]{:S(2)}) copy-start(f32[64]{0:T(128)} %param.14) | copy-start | bytes 772
  30.4 4.4 %collective-permute-start.4 = (bf16[64,1,128]{2,0,1:T(8,128)(2,1)S(1)}, bf16[64,1,128]{2,0,1:T(8,128)(2,1)S(1)}, u32[]{:S(2)}, u32[]{:S(2)}) collective-permute-start(bf16[64,1,128]{2,0,1:T(8,128)(2,1)S(1)} %get-tuple-element.11), channel_id=1, source_target_pairs={{0,8},{8,16},{16,24},{1,9},{9,17},{17,25},{2,10},{10,18},{18,26},{... | collective-permute-start | bytes 49160 | tf_op jit(solution)/shard_map/ppermute | solution.py:20
  33.4 4.8 %collective-permute-start.5 = (bf16[64,1,128]{2,0,1:T(8,128)(2,1)S(1)}, bf16[64,1,128]{2,0,1:T(8,128)(2,1)S(1)}, u32[]{:S(2)}, u32[]{:S(2)}) collective-permute-start(bf16[64,1,128]{2,0,1:T(8,128)(2,1)S(1)} %get-tuple-element.12), channel_id=1, source_target_pairs={{8,0},{16,8},{24,16},{9,1},{17,9},{25,17},{10,2},{18,10},{26,18},{... | collective-permute-start | bytes 49160 | tf_op jit(solution)/shard_map/ppermute | solution.py:21
  38.8 6.1 %collective-permute-start.6 = (bf16[64,34,1]{0,1,2:T(8,128)(2,1)S(1)}, bf16[64,34,1]{0,1,2:T(8,128)(2,1)S(1)}, u32[]{:S(2)}, u32[]{:S(2)}) collective-permute-start(bf16[64,34,1]{0,1,2:T(8,128)(2,1)S(1)} %copy.79), channel_id=1, source_target_pairs={{0,1},{1,2},{2,3},{3,4},{4,5},{5,6},{6,7},{8,9},{9,10},{10,11},{11... | collective-permute-start | bytes 13064 | tf_op jit(solution)/shard_map/ppermute | solution.py:20
  43.5 5.6 %collective-permute-start.7 = (bf16[64,34,1]{0,1,2:T(8,128)(2,1)S(1)}, bf16[64,34,1]{0,1,2:T(8,128)(2,1)S(1)}, u32[]{:S(2)}, u32[]{:S(2)}) collective-permute-start(bf16[64,34,1]{0,1,2:T(8,128)(2,1)S(1)} %copy.81), channel_id=1, source_target_pairs={{1,0},{2,1},{3,2},{4,3},{5,4},{6,5},{7,6},{9,8},{10,9},{11,10},{12... | collective-permute-start | bytes 13064 | tf_op jit(solution)/shard_map/ppermute | solution.py:21
  50.2 1.6 %copy-start.4 = (bf16[64,576]{1,0:T(8,128)(2,1)S(1)}, bf16[64,576]{1,0:T(8,128)(2,1)}, u32[]{:S(2)}) copy-start(bf16[64,576]{1,0:T(8,128)(2,1)} %param.15) | copy-start | bytes 221188
  50.3 1.6 %copy-start.9 = (f32[64]{0:T(128)S(1)}, f32[64]{0:T(128)}, u32[]{:S(2)}) copy-start(f32[64]{0:T(128)} %param.16) | copy-start | bytes 772
  51.0 2.1 %copy-start.7 = (bf16[64,1,4]{0,2,1:T(4,128)(2,1)S(1)}, bf16[64,1,4]{0,2,1:T(4,128)(2,1)}, u32[]{:S(2)}) copy-start(bf16[64,1,4]{0,2,1:T(4,128)(2,1)} %param.17) | copy-start | bytes 1540
  51.0 67.1 %copy-start.5 = (bf16[64,256]{1,0:T(8,128)(2,1)S(1)}, bf16[64,256]{1,0:T(8,128)(2,1)}, u32[]{:S(2)}) copy-start(bf16[64,256]{1,0:T(8,128)(2,1)} %param.20) | copy-start | bytes 98308
  51.0 67.6 %copy-start.6 = (bf16[64,256]{1,0:T(8,128)(2,1)S(1)}, bf16[64,256]{1,0:T(8,128)(2,1)}, u32[]{:S(2)}) copy-start(bf16[64,256]{1,0:T(8,128)(2,1)} %param.21) | copy-start | bytes 98308
  51.3 68.1 %copy-start.2 = (bf16[256,256]{1,0:T(8,128)(2,1)S(1)}, bf16[256,256]{1,0:T(8,128)(2,1)}, u32[]{:S(2)}) copy-start(bf16[256,256]{1,0:T(8,128)(2,1)} %param.22) | copy-start | bytes 393220
where the time goes:
time: 121 us; the launch traced here: 120 us
  blocking collectives  65 us (54%)
  starting transfers between devices  18.2 us (15%)
  waiting for transfers between devices  10.8 us (9%)
  other arithmetic  10.2 us (8%)
  local copies, waits for them, and re-layouts  8.8 us (7%)
  matrix products  6.67 us (6%)
    all_gather x1, blocking collectives, on_device(): piece = lax.all_gather(flat, ('row', 'col'), axis=0, tiled=True)  65 us
    ppermute x4, starting transfers between devices, padded_2(): before = lax.ppermute(last, axis, up)  13 us
    ppermute x4, waiting for transfers between devices, padded_2(): after = lax.ppermute(leading, axis, down)  10.8 us
    unnamed x10, other arithmetic  7.76 us
    ppermute x4, starting transfers between devices, padded_2(): after = lax.ppermute(leading, axis, down)  5.15 us
    unnamed x32, local copies, waits for them, and re-layouts  4.69 us
    dot_general x2, matrix products, conv_layer(): jnp.einsum('ok,khw->ohw', weight, stacked, preferred_element_type=jnp.flo...  4.41 us
  transfers between devices with their start and end apart: 8, of which 4 were waited for; matrix products, arithmetic and copies ran while one was open for 5% of the time, Pallas kernels for 0%

commit v1 on v0

v1 whole, which is shorter than its diff:
```python
import functools

import jax
import jax.numpy as jnp
from jax import lax
from jax.experimental import pallas as pl
from jax.experimental.pallas import tpu as pltpu
from jax.sharding import PartitionSpec as P

HEADS = 8
HEAD_DIM = 32
PATCH = 32
QBLOCK = 128
SLOT = 16
MESH = pl.DeviceIdType.MESH
F32 = jnp.float32
BF16 = jnp.bfloat16
SIDES = ((-1, -1), (-1, 1), (0, -1), (0, 1), (1, -1), (1, 1))


def iota(shape, dim):
    return lax.broadcasted_iota(jnp.int32, shape, dim)


def dot(a, b):
    return jnp.dot(a, b, preferred_element_type=F32)


def dot_nt(a, b):
    return lax.dot_general(a, b, (((1,), (1,)), ((), ())), preferred_element_type=F32)


def column(row_vec):
    n = row_vec.shape[1]
    spread = jnp.where(iota((n, n), 0) == iota((n, n), 1), row_vec, 0.0)
    return jnp.sum(spread, axis=1, keepdims=True)


def kernel(
    sizes,
    x_ref,
    conv_one_ref,
    bias_one_ref,
    conv_two_ref,
    bias_two_ref,
    pos_ref,
    embed_ref,
    w_query_ref,
    w_key_ref,
    w_value_ref,
    w_out_ref,
    visible_ref,
    out_ref,
    x3,
    f3,
    w2a,
    w2b,
    pack,
    rows_in,
    packs_in,
    token,
    gathered,
    row_send,
    row_recv,
    pack_send,
    pack_recv,
    tok_send,
    tok_recv,
):
    n_row, n_col, ch, rows, cols = sizes
    n = n_row * n_col
    r = lax.axis_index("row")
    c = lax.axis_index("col")
    me = r * n_col + c
    owned = out_ref.shape[0]
    e = out_ref.shape[1]

    def place(d):
        return (lax.div(d, n_col), lax.rem(d, n_col))

    barrier = pltpu.get_barrier_semaphore()

    def greet(k, carry):
        pl.semaphore_signal(
            barrier, inc=1, device_id=place(lax.rem(me + k, n)), device_id_type=MESH
        )
        return carry

    lax.fori_loop(1, n, greet, 0)

    lane = iota((ch, cols), 1)
    group = lax.rem(lane + 2, cols) // 4

    def pack_rows(i, acc):
        for j in range(4):
            h = i * 4 + j
            part = x_ref[pl.ds(pl.multiple_of(h * ch, ch), ch), :].astype(F32)
            acc = jnp.where(group == h, pltpu.roll(part, h * 4, 1), acc)
        return acc

    pack[...] = lax.fori_loop(0, rows // 4, pack_rows, jnp.zeros((ch, cols), F32)).astype(BF16)

    for conv_ref, w2 in ((conv_one_ref, w2a), (conv_two_ref, w2b)):
        w = conv_ref[...]
        pad = jnp.zeros((ch, 3 * ch), BF16)
        w2[0:ch, :] = jnp.concatenate([w, pad], axis=1)
        w2[ch : 2 * ch, :] = jnp.concatenate([pad, w], axis=1)

    pl.semaphore_wait(barrier, n - 1)

    def row_copy(up):
        return pltpu.make_async_remote_copy(
            src_ref=x_ref.at[pl.ds(0 if up else (rows - 2) * ch, 2 * ch)],
            dst_ref=rows_in.at[1 if up else 0],
            send_sem=row_send.at[0 if up else 1],
            recv_sem=row_recv.at[1 if up else 0],
            device_id=(r - 1 if up else r + 1, c),
            device_id_type=MESH,
        )

    def pack_copy(index):
        dr, dc = SIDES[index]
        there = SIDES.index((-dr, -dc))
        return pltpu.make_async_remote_copy(
            src_ref=pack,
            dst_ref=packs_in.at[there],
            send_sem=pack_send.at[index],
            recv_sem=pack_recv.at[there],
            device_id=(r + dr, c + dc),
            device_id_type=MESH,
        )

    def row_there(up):
        return r > 0 if up else r < n_row - 1

    def side_there(index):
        dr, dc = SIDES[index]
        ok = c > 0 if dc < 0 else c < n_col - 1
        if dr:
            ok = jnp.logical_and(ok, row_there(dr < 0))
        return ok

    for index in (2, 3, 0, 1, 4, 5):
        pl.when(side_there(index))(lambda index=index: pack_copy(index).start())
    for up in (True, False):
        pl.when(row_there(up))(lambda up=up: row_copy(up).start())

    pick = iota((owned, embed_ref.shape[0]), 1) == me * owned + iota((owned, embed_ref.shape[0]), 0)
    own = dot(pick.astype(F32).astype(BF16), embed_ref[...]).astype(BF16)
    query = dot(own, w_query_ref[...]).astype(BF16).astype(F32)
    tall = (HEADS * owned, e)
    own_head = iota(tall, 0) // owned == iota(tall, 1) // HEAD_DIM
    heads = jnp.where(own_head, jnp.concatenate([query] * HEADS, axis=0), 0.0).astype(BF16)
    wide = (visible_ref.shape[1], n * SLOT)
    local_count = pos_ref.shape[1]
    spread = jnp.logical_and(
        iota(wide, 1) // SLOT == iota(wide, 0), lax.rem(iota(wide, 1), SLOT) < local_count
    )
    blocks = visible_ref.shape
    mine = iota(blocks, 0) == me * owned // QBLOCK
    seen_row = jnp.sum(jnp.where(mine, visible_ref[...], 0).astype(F32), axis=0, keepdims=True)
    seen = dot(
        jnp.broadcast_to(seen_row, (8, blocks[1])).astype(BF16), spread.astype(F32).astype(BF16)
    )[0:1] > 0.5

    for index in range(6):

        @pl.when(side_there(index))
        def _(index=index):
            back = SIDES.index((-SIDES[index][0], -SIDES[index][1]))
            pack_copy(index).wait_send()
            pack_copy(back).wait_recv()

        @pl.when(jnp.logical_not(side_there(index)))
        def _(index=index):
            packs_in[index] = jnp.zeros((ch, cols), BF16)

    for up in (True, False):

        @pl.when(row_there(up))
        def _(up=up):
            row_copy(up).wait_send()
            row_copy(not up).wait_recv()

        @pl.when(jnp.logical_not(row_there(up)))
        def _(up=up):
            rows_in[0 if up else 1] = jnp.zeros((2 * ch, cols), BF16)

    from_right = lax.rem(lane, 4) < 2

    def rim(dr):
        left = packs_in[SIDES.index((dr, -1))].astype(F32)
        right = packs_in[SIDES.index((dr, 1))].astype(F32)
        return jnp.where(from_right, right, left)

    def fill(slot, center, rim_rolled):
        full = jnp.concatenate([center.astype(F32), rim_rolled], axis=1)
        base = pl.multiple_of(slot * (3 * ch), 3 * ch)
        x3[pl.ds(base, ch), :] = pltpu.roll(full, 1, 1).astype(BF16)
        x3[pl.ds(base + ch, ch), :] = full.astype(BF16)
        x3[pl.ds(base + 2 * ch, ch), :] = pltpu.roll(full, 2 * cols - 1, 1).astype(BF16)

    beside = rim(0)

    def fill_rows(i, carry):
        for j in range(4):
            h = i * 4 + j
            center = x_ref[pl.ds(pl.multiple_of(h * ch, ch), ch), :]
            fill(h + 2, center, pltpu.roll(beside, lax.rem(cols - 4 * h, cols), 1))
        return carry

    lax.fori_loop(0, rows // 4, fill_rows, 0)
    above, below = rim(-1), rim(1)
    for j in range(2):
        h = rows - 2 + j
        fill(j, rows_in[0, j * ch : (j + 1) * ch], pltpu.roll(above, (cols - 4 * h) % cols, 1))
        fill(rows + 2 + j, rows_in[1, j * ch : (j + 1) * ch], pltpu.roll(below, (cols - 4 * j) % cols, 1))

    bias_one = column(bias_one_ref[...])
    bias_two = column(bias_two_ref[...])
    bias_one = jnp.concatenate([bias_one, bias_one], axis=0)
    bias_two = jnp.concatenate([bias_two, bias_two], axis=0)
    lanes = iota((1, 2 * cols), 1)
    outside = jnp.logical_or(
        jnp.logical_and(lanes == 2 * cols - 1, c == 0),
        jnp.logical_and(lanes == cols, c == n_col - 1),
    )
    inside = jnp.logical_not(outside)
    half_row = iota((2 * ch, 1), 0) // ch
    lowest = jnp.where(r == 0, 0, -1)
    highest = jnp.where(r == n_row - 1, rows - 1, rows)
    half = rows // 2

    def first_pair(g, slot, side):
        base = pl.multiple_of(g * (6 * ch), 6 * ch)
        acc = dot(w2a[...], x3[pl.ds(base, 12 * ch), :])
        local = 2 * g - 1 + half_row
        keep = jnp.logical_and(jnp.logical_and(local >= lowest, local <= highest), inside)
        acc = jnp.where(keep, jnp.maximum(acc + bias_one, 0.0), 0.0)
        taps = (
            pltpu.roll(acc, 1, 1)[:, :cols].astype(BF16),
            acc[:, :cols].astype(BF16),
            pltpu.roll(acc, 2 * cols - 1, 1)[:, :cols].astype(BF16),
        )
        start = pl.multiple_of(slot * (6 * ch), 6 * ch)
        for o in range(2):
            for t in range(3):
                f3[pl.ds(start + (3 * o + t) * ch, ch), side * cols : (side + 1) * cols] = taps[t][
                    o * ch : (o + 1) * ch
                ]

    def first_step(i, carry):
        first_pair(i, i, 0)
        first_pair(i + half // 2, i, 1)
        return carry

    lax.fori_loop(0, half // 2 + 1, first_step, 0)

    def second_step(j, acc):
        base = pl.multiple_of(j * (6 * ch), 6 * ch)
        return acc + jnp.maximum(dot(w2b[...], f3[pl.ds(base, 12 * ch), :]) + bias_two, 0.0)

    total = lax.fori_loop(0, half // 2, second_step, jnp.zeros((2 * ch, 2 * cols), F32))
    total = total[:ch] + total[ch:]
    total = total[:, :cols] + total[:, cols:]
    high = total.astype(BF16)
    low = (total - high.astype(F32)).astype(BF16)
    pool = (iota((SLOT, cols), 1) // PATCH == iota((SLOT, cols), 0)).astype(F32).astype(BF16)
    pooled = (dot_nt(pool, high) + dot_nt(pool, low)) * (1.0 / (PATCH * PATCH))
    shift = (iota((SLOT, local_count), 1) == iota((SLOT, local_count), 0)).astype(F32).astype(BF16)
    tokens = pooled + dot_nt(shift, pos_ref[...])
    tokens = jnp.concatenate([tokens, jnp.zeros((SLOT, 128 - ch), F32)], axis=1).astype(BF16)
    token[...] = tokens
    gathered[pl.ds(pl.multiple_of(me * SLOT, SLOT), SLOT), :] = tokens

    def token_copy(k, sender):
        return pltpu.make_async_remote_copy(
            src_ref=token,
            dst_ref=gathered.at[pl.ds(pl.multiple_of(sender * SLOT, SLOT), SLOT)],
            send_sem=tok_send.at[k],
            recv_sem=tok_recv.at[sender],
            device_id=place(lax.rem(me + k, n)),
            device_id_type=MESH,
        )

    def push(k, carry):
        token_copy(k, me).start()
        return carry

    def take(k, carry):
        token_copy(k, me).wait_send()
        token_copy(k, lax.rem(me + n - k, n)).wait_recv()
        return carry

    lax.fori_loop(1, n, push, 0)
    lax.fori_loop(1, n, take, 0)

    every = gathered[...][:, :ch]
    keys = dot(every, w_key_ref[...]).astype(BF16)
    values = dot(every, w_value_ref[...]).astype(BF16)
    score = dot_nt(heads, keys) * (1.0 / HEAD_DIM**0.5)
    peak = jnp.max(jnp.where(seen, score, -1e30), axis=1, keepdims=True)
    weight = jnp.where(seen, jnp.exp(score - peak), 0.0)
    norm = jnp.sum(weight, axis=1, keepdims=True)
    mixed = dot(weight.astype(BF16), values) / norm
    mixed = jnp.where(own_head, mixed, 0.0)
    attended = mixed[0:owned]
    for h in range(1, HEADS):
        attended = attended + mixed[h * owned : (h + 1) * owned]
    out_ref[...] = dot(attended.astype(BF16), w_out_ref[...]).astype(BF16)


def on_device(
    raster,
    conv_one,
    bias_one,
    conv_two,
    bias_two,
    pos_embed,
    query_embed,
    w_query,
    w_key,
    w_value,
    w_out,
    visible,
):
    ch, rows, cols = raster.shape
    n_row, n_col = lax.axis_size("row"), lax.axis_size("col")
    n = n_row * n_col
    owned = query_embed.shape[0] // n
    e = query_embed.shape[1]
    flat = raster.transpose(1, 0, 2).reshape(rows * ch, cols)
    vmem = pl.BlockSpec(memory_space=pltpu.VMEM)
    dma = pltpu.SemaphoreType.DMA
    return pl.pallas_call(
        functools.partial(kernel, (n_row, n_col, ch, rows, cols)),
        out_shape=jax.ShapeDtypeStruct((owned, e), BF16),
        in_specs=[vmem] * 12,
        out_specs=vmem,
        scratch_shapes=[
            pltpu.VMEM(((rows + 4) * 3 * ch, 2 * cols), BF16),
            pltpu.VMEM(((rows // 2 + 2) * 3 * ch, 2 * cols), BF16),
            pltpu.VMEM((2 * ch, 12 * ch), BF16),
            pltpu.VMEM((2 * ch, 12 * ch), BF16),
            pltpu.VMEM((ch, cols), BF16),
            pltpu.VMEM((2, 2 * ch, cols), BF16),
            pltpu.VMEM((6, ch, cols), BF16),
            pltpu.VMEM((SLOT, 128), BF16),
            pltpu.VMEM((n * SLOT, 128), BF16),
            dma((2,)),
            dma((2,)),
            dma((6,)),
            dma((6,)),
            dma((n,)),
            dma((n,)),
        ],
        compiler_params=pltpu.CompilerParams(
            collective_id=0, has_side_effects=True, vmem_limit_bytes=40 * 1024 * 1024
        ),
        cost_estimate=pl.CostEstimate(flops=1_000_000_000, bytes_accessed=2_000_000, transcendentals=0),
    )(
        flat,
        conv_one,
        bias_one.reshape(1, ch),
        conv_two,
        bias_two.reshape(1, ch),
        pos_embed.reshape(ch, -1),
        query_embed,
        w_query,
        w_key,
        w_value,
        w_out,
        visible,
    )


def solution(mesh):
    tile = P(None, "row", "col")
    in_specs = (tile, P(), P(), P(), P(), tile, P(), P(), P(), P(), P(), P())
    return jax.shard_map(
        on_device,
        mesh=mesh,
        in_specs=in_specs,
        out_specs=P(("row", "col"), None),
        check_vma=False,
    )
```

time: 121 us -> 27.6 us (0.23)
  blocking collectives: 65 us -> 0 us
  Pallas kernels: 0 us -> 23.9 us
  starting transfers between devices: 18.2 us -> 0 us
  waiting for transfers between devices: 10.8 us -> 0 us
  other arithmetic: 10.2 us -> 0 us
  matrix products: 6.67 us -> 0 us
  local copies, waits for them, and re-layouts: 8.8 us -> 3.39 us
    all_gather x1 -> x0, blocking collectives: 65 us -> none  [on_device(): piece = lax.all_gather(flat, ('row', 'col'), axis=0, tiled=True)]
    pallas_call x0 -> x1, Pallas kernels: none -> 23.9 us  [on_device(): pl.pallas_call(functools.partial(kernel, (n_row, n_col, ch, rows, cols)),...]
    ppermute x8 -> x0, starting transfers between devices: 18.2 us -> none  [the longest x4 13 us: padded_2(): before = lax.ppermute(last, axis, up)]
    ppermute x8 -> x0, waiting for transfers between devices: 10.8 us -> none  [the longest x4 10.8 us: padded_2(): after = lax.ppermute(leading, axis, down)]
    unnamed x10 -> x0, other arithmetic: 7.76 us -> none
    dot_general x8 -> x0, matrix products: 6.67 us -> none  [the longest x2 4.41 us: conv_layer(): jnp.einsum('ok,khw->ohw', weight, stacked, preferred_element_type=jnp.flo...]
    unnamed x32 -> x24, local copies, waits for them, and re-layouts: 4.69 us -> 2.02 us
    concatenate x3 -> x0, other arithmetic: 2.1 us -> none  [the longest x1 1.23 us: conv_layer(): stacked = jnp.concatenate(taps, 0)]
  transfers between devices with their start and end apart: 8 -> 0, of which waited for: 4 -> 0; matrix products, arithmetic and copies ran while one was open for 5% -> 0% of each run, Pallas kernels for 0% -> 0%
where the time goes in v1:
time: 27.6 us; the launch traced here: 27.4 us
  Pallas kernels  23.9 us (87%)
  local copies, waits for them, and re-layouts  3.39 us (12%)
    pallas_call x1, Pallas kernels, on_device(): pl.pallas_call(functools.partial(kernel, (n_row, n_col, ch, rows, cols)),...  23.9 us
    unnamed x24, local copies, waits for them, and re-layouts  2.02 us
    transpose x1, local copies, waits for them, and re-layouts, on_device(): flat = raster.transpose(1, 0, 2).reshape(rows * ch, cols)  1.37 us

profile of v1, /device:TPU:0, one launch (start us, length us, event | category | flops | bytes accessed | tf_op | source)
XLA Modules:
  0.0 27.4 jit_solution(13184478971980199969)
XLA Ops:
  0.0 0.7 %copy-done.10 = bf16[64,1,4]{0,2,1:T(4,128)(2,1)S(1)} copy-done((bf16[64,1,4]{0,2,1:T(4,128)(2,1)S(1)}, bf16[64,1,4]{0,2,1:T(4,128)(2,1)}, u32[]{:S(2)}) %copy-start.10) | copy-done | bytes 536
  0.7 0.1 copy.14
  0.8 0.0 copy-start.1
  0.8 0.0 copy-start.2
  0.8 0.0 copy-start.3
  0.8 0.0 copy-start.4
  0.8 0.0 copy-start.5
  0.9 0.0 copy-start.6
  0.9 0.0 copy-start.9
  0.9 1.4 %copy.13 = bf16[32,64,128]{2,1,0:T(8,128)(2,1)S(1)} copy(bf16[32,64,128]{2,0,1:T(8,128)(2,1)} %bitcast.9) | data formatting | bytes 1048576 | tf_op jit(solution)/shard_map/transpose | solution.py:332
  2.3 0.0 copy-start.7
  2.3 0.0 copy-start.8
  2.3 0.0 copy-done
  2.3 0.0 copy-done.1
  2.3 0.0 copy-done.2
  2.3 0.0 copy-done.3
  2.3 0.0 copy-done.4
  2.3 0.0 copy-done.5
  2.3 0.0 copy-done.6
  2.3 0.0 copy-done.9
  2.4 0.6 %copy-done.7 = s32[2,32]{1,0:T(2,128)S(1)} copy-done((s32[2,32]{1,0:T(2,128)S(1)}, s32[2,32]{1,0:T(2,128)}, u32[]{:S(2)}) %copy-start.7) | copy-done | bytes 280
  2.9 0.0 copy-done.8
  2.9 23.9 %shard_map.118 = bf16[8,256]{1,0:T(8,128)(2,1)S(1)} custom-call(bf16[2048,128]{1,0:T(8,128)(2,1)S(1)} %bitcast.5, bf16[64,576]{1,0:T(8,128)(2,1)S(1)} %copy-done.3, f32[1,64]{1,0:T(1,128)S(1)} %bitcast.7, bf16[64,576]{1,0:T(8,128)(2,1)S(1)} %copy-done.4, f32[1,64]{1,0:T(1,128)S(1)} %bitcast.8, bf16[64,4]{1,0:T(8,128)(2,1)S(1)} %bitcast.6, ...), custom_call_target="tpu_custom_call" | custom-call | flops 1000000000 | bytes 2000000 | tf_op jit(solution)/shard_map/pallas_call | solution.py:335
  26.8 0.6 %copy.16 = bf16[8,256]{1,0:T(8,128)(2,1)} copy(bf16[8,256]{1,0:T(8,128)(2,1)S(1)} %shard_map.118) | data formatting | bytes 8192
  (2 shorter events, 0.0 us)
Async XLA Ops:
  0.0 0.7 %copy-start.10 = (bf16[64,1,4]{0,2,1:T(4,128)(2,1)S(1)}, bf16[64,1,4]{0,2,1:T(4,128)(2,1)}, u32[]{:S(2)}) copy-start(bf16[64,1,4]{0,2,1:T(4,128)(2,1)} %param.17) | copy-start | bytes 1540
  0.8 1.5 %copy-start = (bf16[256,256]{1,0:T(8,128)(2,1)S(1)}, bf16[256,256]{1,0:T(8,128)(2,1)}, u32[]{:S(2)}) copy-start(bf16[256,256]{1,0:T(8,128)(2,1)} %embed_ref.1) | copy-start | bytes 393220
  0.8 1.5 %copy-start.1 = (bf16[256,256]{1,0:T(8,128)(2,1)S(1)}, bf16[256,256]{1,0:T(8,128)(2,1)}, u32[]{:S(2)}) copy-start(bf16[256,256]{1,0:T(8,128)(2,1)} %w_query_ref.1) | copy-start | bytes 393220
  0.8 1.5 %copy-start.2 = (bf16[256,256]{1,0:T(8,128)(2,1)S(1)}, bf16[256,256]{1,0:T(8,128)(2,1)}, u32[]{:S(2)}) copy-start(bf16[256,256]{1,0:T(8,128)(2,1)} %w_out_ref.1) | copy-start | bytes 393220
  0.8 1.5 %copy-start.3 = (bf16[64,576]{1,0:T(8,128)(2,1)S(1)}, bf16[64,576]{1,0:T(8,128)(2,1)}, u32[]{:S(2)}) copy-start(bf16[64,576]{1,0:T(8,128)(2,1)} %conv_one_ref.1) | copy-start | bytes 221188
  0.8 1.5 %copy-start.4 = (bf16[64,576]{1,0:T(8,128)(2,1)S(1)}, bf16[64,576]{1,0:T(8,128)(2,1)}, u32[]{:S(2)}) copy-start(bf16[64,576]{1,0:T(8,128)(2,1)} %conv_two_ref.1) | copy-start | bytes 221188
  0.8 1.5 %copy-start.5 = (bf16[64,256]{1,0:T(8,128)(2,1)S(1)}, bf16[64,256]{1,0:T(8,128)(2,1)}, u32[]{:S(2)}) copy-start(bf16[64,256]{1,0:T(8,128)(2,1)} %w_key_ref.1) | copy-start | bytes 98308
  0.9 1.5 %copy-start.6 = (bf16[64,256]{1,0:T(8,128)(2,1)S(1)}, bf16[64,256]{1,0:T(8,128)(2,1)}, u32[]{:S(2)}) copy-start(bf16[64,256]{1,0:T(8,128)(2,1)} %w_value_ref.1) | copy-start | bytes 98308
  0.9 1.5 %copy-start.9 = (f32[64]{0:T(128)S(1)}, f32[64]{0:T(128)}, u32[]{:S(2)}) copy-start(f32[64]{0:T(128)} %param.16) | copy-start | bytes 772
  2.3 0.7 %copy-start.7 = (s32[2,32]{1,0:T(2,128)S(1)}, s32[2,32]{1,0:T(2,128)}, u32[]{:S(2)}) copy-start(s32[2,32]{1,0:T(2,128)} %visible_ref.1) | copy-start | bytes 772
  2.3 0.7 %copy-start.8 = (f32[64]{0:T(128)S(1)}, f32[64]{0:T(128)}, u32[]{:S(2)}) copy-start(f32[64]{0:T(128)} %param.14) | copy-start | bytes 772

commit v2 on v1

v2 whole, which is shorter than its diff:
```python
import functools

import jax
import jax.numpy as jnp
from jax import lax
from jax.experimental import pallas as pl
from jax.experimental.pallas import tpu as pltpu
from jax.sharding import PartitionSpec as P

HEADS = 8
HEAD_DIM = 32
PATCH = 32
QBLOCK = 128
SLOT = 16
MESH = pl.DeviceIdType.MESH
F32 = jnp.float32
BF16 = jnp.bfloat16
SIDES = ((0, -1), (0, 1), (-1, 0), (1, 0), (-1, -1), (-1, 1), (1, -1), (1, 1))


def iota(shape, dim):
    return lax.broadcasted_iota(jnp.int32, shape, dim)


def dot(a, b):
    return jnp.dot(a, b, preferred_element_type=F32)


def dot_nt(a, b):
    return lax.dot_general(a, b, (((1,), (1,)), ((), ())), preferred_element_type=F32)


def column(row_vec):
    n = row_vec.shape[1]
    spread = jnp.where(iota((n, n), 0) == iota((n, n), 1), row_vec, 0.0)
    return jnp.sum(spread, axis=1, keepdims=True)


def kernel(sizes, *refs):
    n_row, n_col, ch, rows, cols = sizes
    operands, out_ref, local = refs[:12], refs[12], refs[13:25]
    (xt, x3, f3, w2a, w2b, pack, rows_in, packs_in, token, gathered) = refs[25:35]
    (load_sem, row_send, row_recv, pack_send, pack_recv, tok_send, tok_recv) = refs[35:]
    (
        raster_ref,
        conv_one_ref,
        bias_one_ref,
        conv_two_ref,
        bias_two_ref,
        pos_ref,
        embed_ref,
        w_query_ref,
        w_key_ref,
        w_value_ref,
        w_out_ref,
        visible_ref,
    ) = local
    n = n_row * n_col
    r = lax.axis_index("row")
    c = lax.axis_index("col")
    me = r * n_col + c
    owned = out_ref.shape[0]
    e = out_ref.shape[1]
    half = rows // 2

    loads = [
        pltpu.make_async_copy(operands[i], local[i], load_sem.at[i]) for i in range(len(operands))
    ]
    loads[0].start()

    def away(i, j):
        rr, cc = r + i, c + j
        return (jnp.where(rr >= n_row, rr - n_row, rr), jnp.where(cc >= n_col, cc - n_col, cc))

    def others(body):
        for i in range(n_row):
            lax.fori_loop(0 if i else 1, n_col, lambda j, carry, i=i: body(i, j, carry), 0)

    barrier = pltpu.get_barrier_semaphore()

    def greet(i, j, carry):
        pl.semaphore_signal(barrier, inc=1, device_id=away(i, j), device_id_type=MESH)
        return carry

    others(greet)
    for copy in loads[1:]:
        copy.start()

    loads[0].wait()

    def turn(i, carry):
        start = pl.multiple_of(i * 16, 16)
        part = raster_ref[pl.ds(start, 16)].astype(F32)
        part = jnp.transpose(part, (1, 0, 2)).astype(BF16)
        xt[:, pl.ds(start, 16), :] = part
        return carry

    lax.fori_loop(0, ch // 16, turn, 0)

    lane = iota((ch, cols), 1)
    group = lax.rem(lane + 2, cols) // 4

    def pack_rows(i, acc):
        for j in range(4):
            h = i * 4 + j
            acc = jnp.where(group == h, pltpu.roll(xt[h].astype(F32), h * 4, 1), acc)
        return acc

    packed = lax.fori_loop(0, rows // 4, pack_rows, jnp.zeros((ch, cols), F32))
    pack[...] = packed.astype(BF16)

    pl.semaphore_wait(barrier, n - 1)

    def row_copy(up):
        return pltpu.make_async_remote_copy(
            src_ref=xt.at[pl.ds(0 if up else rows - 2, 2)],
            dst_ref=rows_in.at[1 if up else 0],
            send_sem=row_send.at[0 if up else 1],
            recv_sem=row_recv.at[1 if up else 0],
            device_id=(r - 1 if up else r + 1, c),
            device_id_type=MESH,
        )

    def pack_copy(index):
        dr, dc = SIDES[index]
        there = SIDES.index((-dr, -dc))
        return pltpu.make_async_remote_copy(
            src_ref=pack,
            dst_ref=packs_in.at[there],
            send_sem=pack_send.at[index],
            recv_sem=pack_recv.at[there],
            device_id=(r + dr, c + dc),
            device_id_type=MESH,
        )

    def row_there(up):
        return r > 0 if up else r < n_row - 1

    def side_there(index):
        dr, dc = SIDES[index]
        ok = None
        if dr:
            ok = row_there(dr < 0)
        if dc:
            beside = c > 0 if dc < 0 else c < n_col - 1
            ok = beside if ok is None else jnp.logical_and(ok, beside)
        return ok

    for up in (True, False):
        pl.when(row_there(up))(lambda up=up: row_copy(up).start())
    for index in range(8):
        pl.when(side_there(index))(lambda index=index: pack_copy(index).start())

    for copy in loads[1:]:
        copy.wait()

    for conv_ref, w2 in ((conv_one_ref, w2a), (conv_two_ref, w2b)):
        w = conv_ref[...]
        pad = jnp.zeros((ch, 3 * ch), BF16)
        w2[0:ch, :] = jnp.concatenate([w, pad], axis=1)
        w2[ch : 2 * ch, :] = jnp.concatenate([pad, w], axis=1)

    pick = iota((owned, embed_ref.shape[0]), 1) == me * owned + iota((owned, embed_ref.shape[0]), 0)
    own = dot(pick.astype(F32).astype(BF16), embed_ref[...]).astype(BF16)
    query = dot(own, w_query_ref[...]).astype(BF16).astype(F32)
    tall = (HEADS * owned, e)
    own_head = iota(tall, 0) // owned == iota(tall, 1) // HEAD_DIM
    heads = jnp.where(own_head, jnp.concatenate([query] * HEADS, axis=0), 0.0).astype(BF16)
    wide = (visible_ref.shape[1], n * SLOT)
    local_count = pos_ref.shape[0]
    spread = jnp.logical_and(
        iota(wide, 1) // SLOT == iota(wide, 0), lax.rem(iota(wide, 1), SLOT) < local_count
    )
    blocks = visible_ref.shape
    mine = iota(blocks, 0) == me * owned // QBLOCK
    seen_row = jnp.sum(jnp.where(mine, visible_ref[...], 0).astype(F32), axis=0, keepdims=True)
    seen = dot(
        jnp.broadcast_to(seen_row, (8, blocks[1])).astype(BF16), spread.astype(F32).astype(BF16)
    )[0:1] > 0.5

    bias_one = column(bias_one_ref[...])
    bias_two = column(bias_two_ref[...])
    bias_pair = jnp.concatenate([bias_one, bias_one], axis=0)
    bias_two = jnp.concatenate([bias_two, bias_two], axis=0)

    for up in (True, False):

        @pl.when(row_there(up))
        def _(up=up):
            row_copy(up).wait_send()
            row_copy(not up).wait_recv()

        @pl.when(jnp.logical_not(row_there(up)))
        def _(up=up):
            rows_in[0 if up else 1] = jnp.zeros((2, ch, cols), BF16)

    for index in range(8):

        @pl.when(side_there(index))
        def _(index=index):
            back = SIDES.index((-SIDES[index][0], -SIDES[index][1]))
            pack_copy(index).wait_send()
            pack_copy(back).wait_recv()

        @pl.when(jnp.logical_not(side_there(index)))
        def _(index=index):
            packs_in[index] = jnp.zeros((ch, cols), BF16)

    at_left = lax.rem(lane, 4) == 0

    def turned(x, shift):
        return pltpu.roll(x, shift % cols, 1)

    def rim(dr):
        left = packs_in[SIDES.index((dr, -1))].astype(F32)
        right = packs_in[SIDES.index((dr, 1))].astype(F32)
        mid = packs_in[SIDES.index((dr, 0))].astype(F32) if dr else packed
        return (
            jnp.where(at_left, turned(left, 2), mid),
            jnp.where(at_left, turned(left, 1), turned(right, -1)),
            jnp.where(at_left, mid, turned(right, -2)),
        )

    above, beside, below = rim(-1), rim(0), rim(1)

    def fill(slot, side, center, edge):
        left = jnp.where(lane == 0, edge, pltpu.roll(center, 1, 1))
        right = jnp.where(lane == cols - 1, edge, pltpu.roll(center, cols - 1, 1))
        base = slot * (3 * ch)
        if not isinstance(slot, int):
            base = pl.multiple_of(base, 3 * ch)
        where = slice(side * cols, (side + 1) * cols)
        for t, part in enumerate((left, center, right)):
            x3[pl.ds(base + t * ch, ch), where] = part.astype(BF16)

    def fill_rows(i, carry):
        for j in range(2):
            for side in range(2):
                s = i * 2 + j
                h = s + side * (half - 2)
                fill(s + 2 - 2 * side, side, xt[h].astype(F32), pltpu.roll(beside[1], lax.rem(cols - 4 * h + cols, cols), 1))
        return carry

    lax.fori_loop(0, half // 2 + 1, fill_rows, 0)
    for j in range(2):
        fill(j, 0, rows_in[0, j].astype(F32), turned(above[1], -4 * (rows - 2 + j)))
        fill(half + 2 + j, 1, rows_in[1, j].astype(F32), turned(below[1], -4 * j))

    row_of = lax.rem(lane + 1, cols) // 4
    first_row, last_row = row_of == 0, row_of == rows - 1
    main, extra = [], []
    for t in range(3):
        up_above, up_own = turned(above[t], 4), turned(beside[t], 4)
        main.append(jnp.where(first_row, up_above, up_own))
        extra.append(jnp.where(last_row, up_above, up_own))
    for t in range(3):
        main.append(beside[t])
        extra.append(jnp.where(last_row, above[t], below[t]))
    for t in range(3):
        down_below, down_own = turned(below[t], -4), turned(beside[t], -4)
        main.append(jnp.where(last_row, down_below, down_own))
        extra.append(jnp.where(last_row, down_own, down_below))
    taps = jnp.concatenate(
        [jnp.concatenate(main, axis=0).astype(BF16), jnp.concatenate(extra, axis=0).astype(BF16)], axis=1
    )
    edge = jnp.maximum(dot(conv_one_ref[...], taps) + bias_one, 0.0)
    outside = jnp.logical_or(
        jnp.logical_and(at_left, c == 0), jnp.logical_and(jnp.logical_not(at_left), c == n_col - 1)
    )
    off_grid = jnp.logical_or(
        jnp.logical_and(last_row, r == 0), jnp.logical_and(jnp.logical_not(last_row), r == n_row - 1)
    )
    edge_main = jnp.where(outside, 0.0, edge[:, :cols])
    edge_extra = jnp.where(jnp.logical_or(outside, off_grid), 0.0, edge[:, cols:])

    def put(pair, side, acc, edges):
        for o in range(2):
            part = acc[o * ch : (o + 1) * ch, side * cols : (side + 1) * cols]
            left = jnp.where(lane == 0, edges[o], pltpu.roll(part, 1, 1))
            right = jnp.where(lane == cols - 1, edges[o], pltpu.roll(part, cols - 1, 1))
            base = pair * (6 * ch)
            if not isinstance(pair, int):
                base = pl.multiple_of(base, 6 * ch)
            for t, piece in enumerate((left, part, right)):
                f3[pl.ds(base + (3 * o + t) * ch, ch), side * cols : (side + 1) * cols] = piece.astype(
                    BF16
                )

    def first_pair(i):
        base = i * (6 * ch)
        if not isinstance(i, int):
            base = pl.multiple_of(base, 6 * ch)
        return jnp.maximum(dot(w2a[...], x3[pl.ds(base, 12 * ch), :]) + bias_pair, 0.0)

    def edge_of(h):
        return pltpu.roll(edge_main, lax.rem(2 * cols - 4 * h, cols), 1)

    top = jnp.logical_and(iota((2 * ch, 2 * cols), 0) < ch, iota((2 * ch, 2 * cols), 1) < cols)
    acc = jnp.where(jnp.logical_and(top, r == 0), 0.0, first_pair(0))
    put(0, 0, acc, (turned(edge_extra, -4 * (rows - 1)), turned(edge_main, 0)))
    put(0, 1, acc, (turned(edge_main, -4 * (half - 1)), turned(edge_main, -4 * half)))

    def first_step(i, carry):
        acc = first_pair(i)
        for side in range(2):
            h = 2 * i - 1 + side * half
            put(i, side, acc, (edge_of(h), edge_of(h + 1)))
        return carry

    lax.fori_loop(1, half // 2, first_step, 0)
    bottom = jnp.logical_and(iota((2 * ch, 2 * cols), 0) >= ch, iota((2 * ch, 2 * cols), 1) >= cols)
    acc = jnp.where(jnp.logical_and(bottom, r == n_row - 1), 0.0, first_pair(half // 2))
    put(half // 2, 0, acc, (turned(edge_main, -4 * (half - 1)), turned(edge_main, -4 * half)))
    put(half // 2, 1, acc, (turned(edge_main, -4 * (rows - 1)), turned(edge_extra, 0)))

    def second_step(j, acc):
        base = pl.multiple_of(j * (6 * ch), 6 * ch)
        return acc + jnp.maximum(dot(w2b[...], f3[pl.ds(base, 12 * ch), :]) + bias_two, 0.0)

    total = lax.fori_loop(0, half // 2, second_step, jnp.zeros((2 * ch, 2 * cols), F32))
    total = total[:ch] + total[ch:]
    total = total[:, :cols] + total[:, cols:]
    high = total.astype(BF16)
    low = (total - high.astype(F32)).astype(BF16)
    pool = (iota((SLOT, cols), 1) // PATCH == iota((SLOT, cols), 0)).astype(F32).astype(BF16)
    pooled = (dot_nt(pool, high) + dot_nt(pool, low)) * (1.0 / (PATCH * PATCH))
    shift = jnp.concatenate(
        [pos_ref[...].astype(F32), jnp.zeros((SLOT - local_count, ch), F32)], axis=0
    )
    tokens = jnp.concatenate([pooled + shift, jnp.zeros((SLOT, 128 - ch), F32)], axis=1).astype(BF16)
    token[...] = tokens
    gathered[pl.ds(pl.multiple_of(me * SLOT, SLOT), SLOT), :] = tokens

    def token_copy(i, j, sender):
        return pltpu.make_async_remote_copy(
            src_ref=token,
            dst_ref=gathered.at[pl.ds(pl.multiple_of(sender * SLOT, SLOT), SLOT)],
            send_sem=tok_send.at[i * n_col + j],
            recv_sem=tok_recv.at[sender],
            device_id=away(i, j),
            device_id_type=MESH,
        )

    def push(i, j, carry):
        token_copy(i, j, me).start()
        return carry

    def take(i, j, carry):
        token_copy(i, j, me).wait_send()
        rr, cc = away(i, j)
        token_copy(i, j, rr * n_col + cc).wait_recv()
        return carry

    others(push)
    others(take)

    every = gathered[...][:, :ch]
    keys = dot(every, w_key_ref[...]).astype(BF16)
    values = dot(every, w_value_ref[...]).astype(BF16)
    score = dot_nt(heads, keys) * (1.0 / HEAD_DIM**0.5)
    peak = jnp.max(jnp.where(seen, score, -1e30), axis=1, keepdims=True)
    weight = jnp.where(seen, jnp.exp(score - peak), 0.0)
    norm = jnp.sum(weight, axis=1, keepdims=True)
    mixed = dot(weight.astype(BF16), values) / norm
    mixed = jnp.where(own_head, mixed, 0.0)
    attended = mixed[0:owned]
    for h in range(1, HEADS):
        attended = attended + mixed[h * owned : (h + 1) * owned]
    out_ref[...] = dot(attended.astype(BF16), w_out_ref[...]).astype(BF16)


def on_device(
    raster,
    conv_one,
    bias_one,
    conv_two,
    bias_two,
    pos_embed,
    query_embed,
    w_query,
    w_key,
    w_value,
    w_out,
    visible,
):
    ch, rows, cols = raster.shape
    n_row, n_col = lax.axis_size("row"), lax.axis_size("col")
    n = n_row * n_col
    owned = query_embed.shape[0] // n
    e = query_embed.shape[1]
    dma = pltpu.SemaphoreType.DMA
    operands = (
        raster,
        conv_one,
        bias_one.reshape(1, ch),
        conv_two,
        bias_two.reshape(1, ch),
        pos_embed.transpose(1, 2, 0).reshape(-1, ch),
        query_embed,
        w_query,
        w_key,
        w_value,
        w_out,
        visible,
    )
    wide = 3 * ch, 2 * cols
    return pl.pallas_call(
        functools.partial(kernel, (n_row, n_col, ch, rows, cols)),
        out_shape=jax.ShapeDtypeStruct((owned, e), BF16),
        in_specs=[pl.BlockSpec(memory_space=pl.ANY)] * len(operands),
        out_specs=pl.BlockSpec(memory_space=pltpu.VMEM),
        scratch_shapes=[pltpu.VMEM(x.shape, x.dtype) for x in operands]
        + [
            pltpu.VMEM((rows, ch, cols), BF16),
            pltpu.VMEM(((rows // 2 + 4) * wide[0], wide[1]), BF16),
            pltpu.VMEM(((rows // 2 + 2) * wide[0], wide[1]), BF16),
            pltpu.VMEM((2 * ch, 12 * ch), BF16),
            pltpu.VMEM((2 * ch, 12 * ch), BF16),
            pltpu.VMEM((ch, cols), BF16),
            pltpu.VMEM((2, 2, ch, cols), BF16),
            pltpu.VMEM((8, ch, cols), BF16),
            pltpu.VMEM((SLOT, 128), BF16),
            pltpu.VMEM((n * SLOT, 128), BF16),
            dma((len(operands),)),
            dma((2,)),
            dma((2,)),
            dma((8,)),
            dma((8,)),
            dma((n,)),
            dma((n,)),
        ],
        compiler_params=pltpu.CompilerParams(
            collective_id=0, has_side_effects=True, vmem_limit_bytes=62 * 1024 * 1024
        ),
        cost_estimate=pl.CostEstimate(flops=1_000_000_000, bytes_accessed=2_000_000, transcendentals=0),
    )(*operands)


def solution(mesh):
    tile = P(None, "row", "col")
    in_specs = (tile, P(), P(), P(), P(), tile, P(), P(), P(), P(), P(), P())
    return jax.shard_map(
        on_device,
        mesh=mesh,
        in_specs=in_specs,
        out_specs=P(("row", "col"), None),
        check_vma=False,
    )
```

time: 27.6 us -> 25.1 us (0.909)
  local copies, waits for them, and re-layouts: 3.39 us -> 1.28 us
    transpose x1 -> x0, local copies, waits for them, and re-layouts: 1.37 us -> none  [on_device(): flat = raster.transpose(1, 0, 2).reshape(rows * ch, cols)]
    unnamed x24 -> x1, local copies, waits for them, and re-layouts: 2.02 us -> 1.28 us
where the time goes in v2:
time: 25.1 us; the launch traced here: 25 us
  Pallas kernels  23.7 us (94%)
  local copies, waits for them, and re-layouts  1.28 us (5%)
    pallas_call x1, Pallas kernels, on_device(): pl.pallas_call(functools.partial(kernel, (n_row, n_col, ch, rows, cols)),...  23.7 us
    unnamed x1, local copies, waits for them, and re-layouts  1.28 us

profile of v2, /device:TPU:0, one launch (start us, length us, event | category | flops | bytes accessed | tf_op | source)
XLA Modules:
  0.0 25.0 jit_solution(4156927168439035969)
XLA Ops:
  0.0 23.7 %shard_map.118 = bf16[8,256]{1,0:T(8,128)(2,1)} custom-call(bf16[64,32,128]{2,1,0:T(8,128)(2,1)} %refs_0_.1, bf16[64,576]{1,0:T(8,128)(2,1)} %refs_1_.1, f32[1,64]{1,0:T(1,128)} %bitcast.6, bf16[64,576]{1,0:T(8,128)(2,1)} %refs_3_.1, f32[1,64]{1,0:T(1,128)} %bitcast.7, bf16[4,64]{1,0:T(4,128)(2,1)} %bitcast.5, bf16[256,256]{1,0:T(8,128)(2,1)} %refs_6_.1, ...), custom_call_target="tpu_custom_call" | custom-call | flops 1000000000 | bytes 2000000 | tf_op jit(solution)/shard_map/pallas_call | solution.py:407
  23.7 1.3 %copy.14 = bf16[8,256]{1,0:T(8,128)(2,1)} copy(bf16[8,256]{1,0:T(8,128)(2,1)} %shard_map.118) | data formatting | bytes 8192

commit v3 on v2

--- a/solution.py
+++ b/solution.py
@@ -39,8 +39,8 @@
 def kernel(sizes, *refs):
     n_row, n_col, ch, rows, cols = sizes
     operands, out_ref, local = refs[:12], refs[12], refs[13:25]
-    (xt, x3, f3, w2a, w2b, pack, rows_in, packs_in, token, gathered) = refs[25:35]
-    (load_sem, row_send, row_recv, pack_send, pack_recv, tok_send, tok_recv) = refs[35:]
+    (xt, x3, raw, f3, w2a, w2b, pack, rows_in, packs_in, token, gathered) = refs[25:36]
+    (load_sem, row_send, row_recv, pack_send, pack_recv, tok_send, tok_recv) = refs[36:]
     (
         raster_ref,
         conv_one_ref,
@@ -63,10 +63,18 @@
     e = out_ref.shape[1]
     half = rows // 2
 
+    chunk = ch // 4
+    raster_loads = [
+        pltpu.make_async_copy(
+            operands[0].at[pl.ds(i * chunk, chunk)], raster_ref.at[pl.ds(i * chunk, chunk)], load_sem.at[i]
+        )
+        for i in range(4)
+    ]
     loads = [
-        pltpu.make_async_copy(operands[i], local[i], load_sem.at[i]) for i in range(len(operands))
+        pltpu.make_async_copy(operands[i], local[i], load_sem.at[i + 3]) for i in range(1, len(operands))
     ]
-    loads[0].start()
+    for copy in raster_loads:
+        copy.start()
 
     def away(i, j):
         rr, cc = r + i, c + j
@@ -83,19 +91,13 @@
         return carry
 
     others(greet)
-    for copy in loads[1:]:
+    for copy in loads:
         copy.start()
 
-    loads[0].wait()
-
-    def turn(i, carry):
-        start = pl.multiple_of(i * 16, 16)
-        part = raster_ref[pl.ds(start, 16)].astype(F32)
-        part = jnp.transpose(part, (1, 0, 2)).astype(BF16)
-        xt[:, pl.ds(start, 16), :] = part
-        return carry
-
-    lax.fori_loop(0, ch // 16, turn, 0)
+    for i, copy in enumerate(raster_loads):
+        copy.wait()
+        part = raster_ref[i * chunk : (i + 1) * chunk].astype(F32)
+        xt[:, i * chunk : (i + 1) * chunk, :] = jnp.transpose(part, (1, 0, 2)).astype(BF16)
 
     lane = iota((ch, cols), 1)
     group = lax.rem(lane + 2, cols) // 4
@@ -151,7 +153,7 @@
     for index in range(8):
         pl.when(side_there(index))(lambda index=index: pack_copy(index).start())
 
-    for copy in loads[1:]:
+    for copy in loads:
         copy.wait()
 
     for conv_ref, w2 in ((conv_one_ref, w2a), (conv_two_ref, w2b)):
@@ -159,6 +161,35 @@
         pad = jnp.zeros((ch, 3 * ch), BF16)
         w2[0:ch, :] = jnp.concatenate([w, pad], axis=1)
         w2[ch : 2 * ch, :] = jnp.concatenate([pad, w], axis=1)
+
+    def fill(slot, side, center):
+        left = jnp.where(lane == 0, 0.0, pltpu.roll(center, 1, 1))
+        right = jnp.where(lane == cols - 1, 0.0, pltpu.roll(center, cols - 1, 1))
+        base = slot * (3 * ch)
+        if not isinstance(slot, int):
+            base = pl.multiple_of(base, 3 * ch)
+        where = slice(side * cols, (side + 1) * cols)
+        for t, part in enumerate((left, center, right)):
+            x3[pl.ds(base + t * ch, ch), where] = part.astype(BF16)
+
+    def fill_rows(i, carry):
+        for j in range(2):
+            for side in range(2):
+                s = i * 2 + j
+                fill(s + 2 - 2 * side, side, xt[s + side * (half - 2)].astype(F32))
+        return carry
+
+    lax.fori_loop(0, half // 2 + 1, fill_rows, 0)
+
+    def first_sums(i, carry):
+        base = i * (6 * ch)
+        out = i * (2 * ch)
+        if not isinstance(i, int):
+            base, out = pl.multiple_of(base, 6 * ch), pl.multiple_of(out, 2 * ch)
+        raw[pl.ds(out, 2 * ch), :] = dot(w2a[...], x3[pl.ds(base, 12 * ch), :])
+        return carry
+
+    lax.fori_loop(1, half // 2, first_sums, 0)
 
     pick = iota((owned, embed_ref.shape[0]), 1) == me * owned + iota((owned, embed_ref.shape[0]), 0)
     own = dot(pick.astype(F32).astype(BF16), embed_ref[...]).astype(BF16)
@@ -166,11 +197,9 @@
     tall = (HEADS * owned, e)
     own_head = iota(tall, 0) // owned == iota(tall, 1) // HEAD_DIM
     heads = jnp.where(own_head, jnp.concatenate([query] * HEADS, axis=0), 0.0).astype(BF16)
-    wide = (visible_ref.shape[1], n * SLOT)
     local_count = pos_ref.shape[0]
-    spread = jnp.logical_and(
-        iota(wide, 1) // SLOT == iota(wide, 0), lax.rem(iota(wide, 1), SLOT) < local_count
-    )
+    wide = (visible_ref.shape[1], n * local_count)
+    spread = iota(wide, 1) // local_count == iota(wide, 0)
     blocks = visible_ref.shape
     mine = iota(blocks, 0) == me * owned // QBLOCK
     seen_row = jnp.sum(jnp.where(mine, visible_ref[...], 0).astype(F32), axis=0, keepdims=True)
@@ -180,7 +209,6 @@
 
     bias_one = column(bias_one_ref[...])
     bias_two = column(bias_two_ref[...])
-    bias_pair = jnp.concatenate([bias_one, bias_one], axis=0)
     bias_two = jnp.concatenate([bias_two, bias_two], axis=0)
 
     for up in (True, False):
@@ -223,28 +251,11 @@
 
     above, beside, below = rim(-1), rim(0), rim(1)
 
-    def fill(slot, side, center, edge):
-        left = jnp.where(lane == 0, edge, pltpu.roll(center, 1, 1))
-        right = jnp.where(lane == cols - 1, edge, pltpu.roll(center, cols - 1, 1))
-        base = slot * (3 * ch)
-        if not isinstance(slot, int):
-            base = pl.multiple_of(base, 3 * ch)
-        where = slice(side * cols, (side + 1) * cols)
-        for t, part in enumerate((left, center, right)):
-            x3[pl.ds(base + t * ch, ch), where] = part.astype(BF16)
-
-    def fill_rows(i, carry):
-        for j in range(2):
-            for side in range(2):
-                s = i * 2 + j
-                h = s + side * (half - 2)
-                fill(s + 2 - 2 * side, side, xt[h].astype(F32), pltpu.roll(beside[1], lax.rem(cols - 4 * h + cols, cols), 1))
-        return carry
-
-    lax.fori_loop(0, half // 2 + 1, fill_rows, 0)
     for j in range(2):
-        fill(j, 0, rows_in[0, j].astype(F32), turned(above[1], -4 * (rows - 2 + j)))
-        fill(half + 2 + j, 1, rows_in[1, j].astype(F32), turned(below[1], -4 * j))
+        fill(j, 0, rows_in[0, j].astype(F32))
+        fill(half + 2 + j, 1, rows_in[1, j].astype(F32))
+    first_sums(0, 0)
+    first_sums(half // 2, 0)
 
     row_of = lax.rem(lane + 1, cols) // 4
     first_row, last_row = row_of == 0, row_of == rows - 1
@@ -260,10 +271,17 @@
         down_below, down_own = turned(below[t], -4), turned(beside[t], -4)
         main.append(jnp.where(last_row, down_below, down_own))
         extra.append(jnp.where(last_row, down_own, down_below))
-    taps = jnp.concatenate(
-        [jnp.concatenate(main, axis=0).astype(BF16), jnp.concatenate(extra, axis=0).astype(BF16)], axis=1
-    )
-    edge = jnp.maximum(dot(conv_one_ref[...], taps) + bias_one, 0.0)
+    zero = jnp.zeros((ch, cols), F32)
+    added = []
+    for part in (main, extra):
+        added.append([])
+        for dy in range(3):
+            mid = part[3 * dy + 1]
+            added[-1] += [jnp.where(at_left, mid, 0.0), zero, jnp.where(at_left, 0.0, mid)]
+    taps = [jnp.concatenate(part, axis=0).astype(BF16) for part in (main, extra, added[0], added[1])]
+    edge = dot(conv_one_ref[...], jnp.concatenate(taps, axis=1))
+    add_main, add_extra = edge[:, 2 * cols : 3 * cols], edge[:, 3 * cols :]
+    edge = jnp.maximum(edge[:, : 2 * cols] + bias_one, 0.0)
     outside = jnp.logical_or(
         jnp.logical_and(at_left, c == 0), jnp.logical_and(jnp.logical_not(at_left), c == n_col - 1)
     )
@@ -273,45 +291,47 @@
     edge_main = jnp.where(outside, 0.0, edge[:, :cols])
     edge_extra = jnp.where(jnp.logical_or(outside, off_grid), 0.0, edge[:, cols:])
 
-    def put(pair, side, acc, edges):
+    ends = jnp.logical_or(lane == 0, lane == cols - 1)
+
+    def put(pair, side, edges, adds, blank=None):
+        base, out = pair * (6 * ch), pair * (2 * ch)
+        if not isinstance(pair, int):
+            base, out = pl.multiple_of(base, 6 * ch), pl.multiple_of(out, 2 * ch)
+        where = slice(side * cols, (side + 1) * cols)
         for o in range(2):
-            part = acc[o * ch : (o + 1) * ch, side * cols : (side + 1) * cols]
+            part = raw[pl.ds(out + o * ch, ch), where] + jnp.where(ends, adds[o], 0.0)
+            part = jnp.maximum(part + bias_one, 0.0)
+            if blank is not None and blank[0] == o:
+                part = jnp.where(blank[1], 0.0, part)
             left = jnp.where(lane == 0, edges[o], pltpu.roll(part, 1, 1))
             right = jnp.where(lane == cols - 1, edges[o], pltpu.roll(part, cols - 1, 1))
-            base = pair * (6 * ch)
-            if not isinstance(pair, int):
-                base = pl.multiple_of(base, 6 * ch)
             for t, piece in enumerate((left, part, right)):
-                f3[pl.ds(base + (3 * o + t) * ch, ch), side * cols : (side + 1) * cols] = piece.astype(
-                    BF16
-                )
-
-    def first_pair(i):
-        base = i * (6 * ch)
-        if not isinstance(i, int):
-            base = pl.multiple_of(base, 6 * ch)
-        return jnp.maximum(dot(w2a[...], x3[pl.ds(base, 12 * ch), :]) + bias_pair, 0.0)
-
-    def edge_of(h):
-        return pltpu.roll(edge_main, lax.rem(2 * cols - 4 * h, cols), 1)
-
-    top = jnp.logical_and(iota((2 * ch, 2 * cols), 0) < ch, iota((2 * ch, 2 * cols), 1) < cols)
-    acc = jnp.where(jnp.logical_and(top, r == 0), 0.0, first_pair(0))
-    put(0, 0, acc, (turned(edge_extra, -4 * (rows - 1)), turned(edge_main, 0)))
-    put(0, 1, acc, (turned(edge_main, -4 * (half - 1)), turned(edge_main, -4 * half)))
+                f3[pl.ds(base + (3 * o + t) * ch, ch), where] = piece.astype(BF16)
+
+    def row_of_edge(x, h):
+        return pltpu.roll(x, lax.rem(2 * cols - 4 * h, cols), 1)
+
+    def both(h):
+        return [(turned(x, -4 * h), turned(x, -4 * (h + 1))) for x in (edge_main, add_main)]
+
+    def joined(first, h_first, second, h_second):
+        return [
+            (turned(a, -4 * h_first), turned(b, -4 * h_second)) for a, b in zip(first, second)
+        ]
+
+    inner, outer = (edge_main, add_main), (edge_extra, add_extra)
+    put(0, 0, *joined(outer, rows - 1, inner, 0), blank=(0, r == 0))
+    put(0, 1, *both(half - 1))
 
     def first_step(i, carry):
-        acc = first_pair(i)
         for side in range(2):
             h = 2 * i - 1 + side * half
-            put(i, side, acc, (edge_of(h), edge_of(h + 1)))
+            put(i, side, *[(row_of_edge(x, h), row_of_edge(x, h + 1)) for x in inner])
         return carry
 
     lax.fori_loop(1, half // 2, first_step, 0)
-    bottom = jnp.logical_and(iota((2 * ch, 2 * cols), 0) >= ch, iota((2 * ch, 2 * cols), 1) >= cols)
-    acc = jnp.where(jnp.logical_and(bottom, r == n_row - 1), 0.0, first_pair(half // 2))
-    put(half // 2, 0, acc, (turned(edge_main, -4 * (half - 1)), turned(edge_main, -4 * half)))
-    put(half // 2, 1, acc, (turned(edge_main, -4 * (rows - 1)), turned(edge_extra, 0)))
+    put(half // 2, 0, *both(half - 1))
+    put(half // 2, 1, *joined(inner, rows - 1, outer, 0), blank=(1, r == n_row - 1))
 
     def second_step(j, acc):
         base = pl.multiple_of(j * (6 * ch), 6 * ch)
@@ -322,12 +342,13 @@
     total = total[:, :cols] + total[:, cols:]
     high = total.astype(BF16)
     low = (total - high.astype(F32)).astype(BF16)
-    pool = (iota((SLOT, cols), 1) // PATCH == iota((SLOT, cols), 0)).astype(F32).astype(BF16)
+    share = SLOT // local_count
+    at = iota((SLOT, cols), 0) - local_count * lax.rem(me, share)
+    pool = (iota((SLOT, cols), 1) // PATCH == at).astype(F32).astype(BF16)
     pooled = (dot_nt(pool, high) + dot_nt(pool, low)) * (1.0 / (PATCH * PATCH))
-    shift = jnp.concatenate(
-        [pos_ref[...].astype(F32), jnp.zeros((SLOT - local_count, ch), F32)], axis=0
-    )
-    tokens = jnp.concatenate([pooled + shift, jnp.zeros((SLOT, 128 - ch), F32)], axis=1).astype(BF16)
+    shift = (iota((SLOT, local_count), 1) == at[:, :local_count]).astype(F32).astype(BF16)
+    tokens = pooled + dot(shift, pos_ref[...])
+    tokens = jnp.concatenate([tokens, jnp.zeros((SLOT, 128 - ch), F32)], axis=1).astype(BF16)
     token[...] = tokens
     gathered[pl.ds(pl.multiple_of(me * SLOT, SLOT), SLOT), :] = tokens
 
@@ -354,7 +375,8 @@
     others(push)
     others(take)
 
-    every = gathered[...][:, :ch]
+    every = gathered[...].astype(F32).reshape(n // share, share, SLOT, 128).sum(axis=1)
+    every = every.reshape(n * local_count, 128).astype(BF16)[:, :ch]
     keys = dot(every, w_key_ref[...]).astype(BF16)
     values = dot(every, w_value_ref[...]).astype(BF16)
     score = dot_nt(heads, keys) * (1.0 / HEAD_DIM**0.5)
@@ -403,16 +425,18 @@
         w_out,
         visible,
     )
+    operands = tuple(pltpu.with_memory_space_constraint(x, pltpu.HBM) for x in operands)
     wide = 3 * ch, 2 * cols
     return pl.pallas_call(
         functools.partial(kernel, (n_row, n_col, ch, rows, cols)),
         out_shape=jax.ShapeDtypeStruct((owned, e), BF16),
-        in_specs=[pl.BlockSpec(memory_space=pl.ANY)] * len(operands),
+        in_specs=[pl.BlockSpec(memory_space=pltpu.HBM)] * len(operands),
         out_specs=pl.BlockSpec(memory_space=pltpu.VMEM),
         scratch_shapes=[pltpu.VMEM(x.shape, x.dtype) for x in operands]
         + [
             pltpu.VMEM((rows, ch, cols), BF16),
             pltpu.VMEM(((rows // 2 + 4) * wide[0], wide[1]), BF16),
+            pltpu.VMEM(((rows // 4 + 1) * 2 * ch, 2 * cols), F32),
             pltpu.VMEM(((rows // 2 + 2) * wide[0], wide[1]), BF16),
             pltpu.VMEM((2 * ch, 12 * ch), BF16),
             pltpu.VMEM((2 * ch, 12 * ch), BF16),
@@ -421,7 +445,7 @@
             pltpu.VMEM((8, ch, cols), BF16),
             pltpu.VMEM((SLOT, 128), BF16),
             pltpu.VMEM((n * SLOT, 128), BF16),
-            dma((len(operands),)),
+            dma((len(operands) + 3,)),
             dma((2,)),
             dma((2,)),
             dma((8,)),
@@ -430,7 +454,7 @@
             dma((n,)),
         ],
         compiler_params=pltpu.CompilerParams(
-            collective_id=0, has_side_effects=True, vmem_limit_bytes=62 * 1024 * 1024
+            collective_id=0, has_side_effects=True, vmem_limit_bytes=32 * 1024 * 1024
         ),
         cost_estimate=pl.CostEstimate(flops=1_000_000_000, bytes_accessed=2_000_000, transcendentals=0),
     )(*operands)

time: 25.1 us -> 21.7 us (0.86)
  Pallas kernels: 23.7 us -> 20.9 us
  local copies, waits for them, and re-layouts: 1.28 us -> 0.6 us
    pallas_call x1, Pallas kernels: 23.7 us -> 20.9 us  [on_device(): pl.pallas_call(functools.partial(kernel, (n_row, n_col, ch, rows, cols)),...]
    unnamed x1, local copies, waits for them, and re-layouts: 1.28 us -> 0.6 us
where the time goes in v3:
time: 21.7 us; the launch traced here: 21.5 us
  Pallas kernels  20.9 us (96%)
  local copies, waits for them, and re-layouts  0.6 us (3%)
    pallas_call x1, Pallas kernels, on_device(): pl.pallas_call(functools.partial(kernel, (n_row, n_col, ch, rows, cols)),...  20.9 us
    unnamed x1, local copies, waits for them, and re-layouts  0.6 us

profile of v3, /device:TPU:0, one launch (start us, length us, event | category | flops | bytes accessed | tf_op | source)
XLA Modules:
  0.0 21.5 jit_solution(9285971752227966569)
XLA Ops:
  0.0 20.9 %shard_map.118 = bf16[8,256]{1,0:T(8,128)(2,1)S(1)} custom-call(bf16[64,32,128]{2,1,0:T(8,128)(2,1)} %refs_0_.1, bf16[64,576]{1,0:T(8,128)(2,1)} %refs_1_.1, f32[1,64]{1,0:T(1,128)} %bitcast.6, bf16[64,576]{1,0:T(8,128)(2,1)} %refs_3_.1, f32[1,64]{1,0:T(1,128)} %bitcast.7, bf16[4,64]{1,0:T(4,128)(2,1)} %bitcast.5, bf16[256,256]{1,0:T(8,128)(2,1)} %refs_6_.1, ...), custom_call_target="tpu_custom_call" | custom-call | flops 1000000000 | bytes 2000000 | tf_op jit(solution)/shard_map/pallas_call | solution.py:430
  20.9 0.6 %copy.14 = bf16[8,256]{1,0:T(8,128)(2,1)} copy(bf16[8,256]{1,0:T(8,128)(2,1)S(1)} %shard_map.118) | data formatting | bytes 8192

commit v4 on v3

--- a/solution.py
+++ b/solution.py
@@ -39,8 +39,9 @@
 def kernel(sizes, *refs):
     n_row, n_col, ch, rows, cols = sizes
     operands, out_ref, local = refs[:12], refs[12], refs[13:25]
-    (xt, x3, raw, f3, w2a, w2b, pack, rows_in, packs_in, token, gathered) = refs[25:36]
-    (load_sem, row_send, row_recv, pack_send, pack_recv, tok_send, tok_recv) = refs[36:]
+    (xt, x3, raw, f3, w2a, w2b, pack, rows_in, packs_in, token, by_row, block, gathered) = refs[25:38]
+    (load_sem, row_send, row_recv, pack_send, pack_recv) = refs[38:43]
+    (up_send, up_recv, side_send, side_recv) = refs[43:]
     (
         raster_ref,
         conv_one_ref,
@@ -76,21 +77,38 @@
     for copy in raster_loads:
         copy.start()
 
-    def away(i, j):
-        rr, cc = r + i, c + j
-        return (jnp.where(rr >= n_row, rr - n_row, rr), jnp.where(cc >= n_col, cc - n_col, cc))
-
-    def others(body):
-        for i in range(n_row):
-            lax.fori_loop(0 if i else 1, n_col, lambda j, carry, i=i: body(i, j, carry), 0)
+    def row_peer(i):
+        rr = r + i
+        return jnp.where(rr >= n_row, rr - n_row, rr)
+
+    def col_peer(j):
+        cc = c + j
+        return jnp.where(cc >= n_col, cc - n_col, cc)
+
+    def row_there(up):
+        return r > 0 if up else r < n_row - 1
+
+    def side_there(index):
+        dr, dc = SIDES[index]
+        ok = None
+        if dr:
+            ok = row_there(dr < 0)
+        if dc:
+            beside = c > 0 if dc < 0 else c < n_col - 1
+            ok = beside if ok is None else jnp.logical_and(ok, beside)
+        return ok
 
     barrier = pltpu.get_barrier_semaphore()
 
-    def greet(i, j, carry):
-        pl.semaphore_signal(barrier, inc=1, device_id=away(i, j), device_id_type=MESH)
-        return carry
-
-    others(greet)
+    def greet(device):
+        pl.semaphore_signal(barrier, inc=1, device_id=device, device_id_type=MESH)
+
+    lax.fori_loop(1, n_col, lambda j, carry: (greet((r, col_peer(j))), carry)[1], 0)
+    lax.fori_loop(1, n_row, lambda i, carry: (greet((row_peer(i), c)), carry)[1], 0)
+    corners = [index for index in range(8) if SIDES[index][0] and SIDES[index][1]]
+    for index in corners:
+        dr, dc = SIDES[index]
+        pl.when(side_there(index))(lambda dr=dr, dc=dc: greet((r + dr, c + dc)))
     for copy in loads:
         copy.start()
 
@@ -111,7 +129,9 @@
     packed = lax.fori_loop(0, rows // 4, pack_rows, jnp.zeros((ch, cols), F32))
     pack[...] = packed.astype(BF16)
 
-    pl.semaphore_wait(barrier, n - 1)
+    high_low = jnp.where(r > 0, 1, 0) + jnp.where(r < n_row - 1, 1, 0)
+    left_right = jnp.where(c > 0, 1, 0) + jnp.where(c < n_col - 1, 1, 0)
+    pl.semaphore_wait(barrier, n_row + n_col - 2 + high_low * left_right)
 
     def row_copy(up):
         return pltpu.make_async_remote_copy(
@@ -135,19 +155,6 @@
             device_id_type=MESH,
         )
 
-    def row_there(up):
-        return r > 0 if up else r < n_row - 1
-
-    def side_there(index):
-        dr, dc = SIDES[index]
-        ok = None
-        if dr:
-            ok = row_there(dr < 0)
-        if dc:
-            beside = c > 0 if dc < 0 else c < n_col - 1
-            ok = beside if ok is None else jnp.logical_and(ok, beside)
-        return ok
-
     for up in (True, False):
         pl.when(row_there(up))(lambda up=up: row_copy(up).start())
     for index in range(8):
@@ -190,22 +197,6 @@
         return carry
 
     lax.fori_loop(1, half // 2, first_sums, 0)
-
-    pick = iota((owned, embed_ref.shape[0]), 1) == me * owned + iota((owned, embed_ref.shape[0]), 0)
-    own = dot(pick.astype(F32).astype(BF16), embed_ref[...]).astype(BF16)
-    query = dot(own, w_query_ref[...]).astype(BF16).astype(F32)
-    tall = (HEADS * owned, e)
-    own_head = iota(tall, 0) // owned == iota(tall, 1) // HEAD_DIM
-    heads = jnp.where(own_head, jnp.concatenate([query] * HEADS, axis=0), 0.0).astype(BF16)
-    local_count = pos_ref.shape[0]
-    wide = (visible_ref.shape[1], n * local_count)
-    spread = iota(wide, 1) // local_count == iota(wide, 0)
-    blocks = visible_ref.shape
-    mine = iota(blocks, 0) == me * owned // QBLOCK
-    seen_row = jnp.sum(jnp.where(mine, visible_ref[...], 0).astype(F32), axis=0, keepdims=True)
-    seen = dot(
-        jnp.broadcast_to(seen_row, (8, blocks[1])).astype(BF16), spread.astype(F32).astype(BF16)
-    )[0:1] > 0.5
 
     bias_one = column(bias_one_ref[...])
     bias_two = column(bias_two_ref[...])
@@ -342,41 +333,82 @@
     total = total[:, :cols] + total[:, cols:]
     high = total.astype(BF16)
     low = (total - high.astype(F32)).astype(BF16)
+    local_count = pos_ref.shape[0]
     share = SLOT // local_count
-    at = iota((SLOT, cols), 0) - local_count * lax.rem(me, share)
+    at = iota((SLOT, cols), 0) - local_count * lax.rem(r, share)
     pool = (iota((SLOT, cols), 1) // PATCH == at).astype(F32).astype(BF16)
     pooled = (dot_nt(pool, high) + dot_nt(pool, low)) * (1.0 / (PATCH * PATCH))
     shift = (iota((SLOT, local_count), 1) == at[:, :local_count]).astype(F32).astype(BF16)
     tokens = pooled + dot(shift, pos_ref[...])
     tokens = jnp.concatenate([tokens, jnp.zeros((SLOT, 128 - ch), F32)], axis=1).astype(BF16)
     token[...] = tokens
-    gathered[pl.ds(pl.multiple_of(me * SLOT, SLOT), SLOT), :] = tokens
-
-    def token_copy(i, j, sender):
+    by_row[pl.ds(pl.multiple_of(r * SLOT, SLOT), SLOT), :] = tokens
+
+    def up_copy(i, sender):
         return pltpu.make_async_remote_copy(
             src_ref=token,
-            dst_ref=gathered.at[pl.ds(pl.multiple_of(sender * SLOT, SLOT), SLOT)],
-            send_sem=tok_send.at[i * n_col + j],
-            recv_sem=tok_recv.at[sender],
-            device_id=away(i, j),
+            dst_ref=by_row.at[pl.ds(pl.multiple_of(sender * SLOT, SLOT), SLOT)],
+            send_sem=up_send.at[i],
+            recv_sem=up_recv.at[sender],
+            device_id=(row_peer(i), c),
             device_id_type=MESH,
         )
 
-    def push(i, j, carry):
-        token_copy(i, j, me).start()
+    depth = n_row * local_count
+
+    def side_copy(j, sender):
+        return pltpu.make_async_remote_copy(
+            src_ref=block,
+            dst_ref=gathered.at[pl.ds(pl.multiple_of(sender * depth, depth), depth)],
+            send_sem=side_send.at[j],
+            recv_sem=side_recv.at[sender],
+            device_id=(r, col_peer(j)),
+            device_id_type=MESH,
+        )
+
+    lax.fori_loop(1, n_row, lambda i, carry: (up_copy(i, r).start(), carry)[1], 0)
+
+    pick = iota((owned, embed_ref.shape[0]), 1) == me * owned + iota((owned, embed_ref.shape[0]), 0)
+    own = dot(pick.astype(F32).astype(BF16), embed_ref[...]).astype(BF16)
+    query = dot(own, w_query_ref[...]).astype(BF16).astype(F32)
+    tall = (HEADS * owned, e)
+    own_head = iota(tall, 0) // owned == iota(tall, 1) // HEAD_DIM
+    heads = jnp.where(own_head, jnp.concatenate([query] * HEADS, axis=0), 0.0).astype(BF16)
+    def take_up(i, carry):
+        up_copy(i, row_peer(i)).wait_recv()
         return carry
 
-    def take(i, j, carry):
-        token_copy(i, j, me).wait_send()
-        rr, cc = away(i, j)
-        token_copy(i, j, rr * n_col + cc).wait_recv()
+    lax.fori_loop(1, n_row, take_up, 0)
+    dense = by_row[...].astype(F32).reshape(n_row // share, share, SLOT, 128).sum(axis=1)
+    dense = dense.reshape(depth, 128).astype(BF16)
+    block[...] = dense
+    lax.fori_loop(1, n_col, lambda j, carry: (side_copy(j, c).start(), carry)[1], 0)
+    gathered[pl.ds(pl.multiple_of(c * depth, depth), depth), :] = dense
+
+    wide = (visible_ref.shape[1], n * local_count)
+    spot = iota(wide, 1) // local_count
+    tile = lax.rem(spot, n_row) * n_col + spot // n_row
+    spread = tile == iota(wide, 0)
+    blocks = visible_ref.shape
+    mine = iota(blocks, 0) == me * owned // QBLOCK
+    seen_row = jnp.sum(jnp.where(mine, visible_ref[...], 0).astype(F32), axis=0, keepdims=True)
+    seen = dot(
+        jnp.broadcast_to(seen_row, (8, blocks[1])).astype(BF16), spread.astype(F32).astype(BF16)
+    )[0:1] > 0.5
+
+    def wait_up(i, carry):
+        up_copy(i, r).wait_send()
         return carry
 
-    others(push)
-    others(take)
-
-    every = gathered[...].astype(F32).reshape(n // share, share, SLOT, 128).sum(axis=1)
-    every = every.reshape(n * local_count, 128).astype(BF16)[:, :ch]
+    def take_side(j, carry):
+        side_copy(j, c).wait_send()
+        side_copy(j, col_peer(j)).wait_recv()
+        return carry
+
+    lax.fori_loop(1, n_row, wait_up, 0)
+    lax.fori_loop(1, n_col, take_side, 0)
+
+    every = gathered[...][:, :ch]
     keys = dot(every, w_key_ref[...]).astype(BF16)
     values = dot(every, w_value_ref[...]).astype(BF16)
     score = dot_nt(heads, keys) * (1.0 / HEAD_DIM**0.5)
@@ -410,6 +442,7 @@
     n = n_row * n_col
     owned = query_embed.shape[0] // n
     e = query_embed.shape[1]
+    local_count = pos_embed.shape[1] * pos_embed.shape[2]
     dma = pltpu.SemaphoreType.DMA
     operands = (
         raster,
@@ -444,14 +477,18 @@
             pltpu.VMEM((2, 2, ch, cols), BF16),
             pltpu.VMEM((8, ch, cols), BF16),
             pltpu.VMEM((SLOT, 128), BF16),
-            pltpu.VMEM((n * SLOT, 128), BF16),
+            pltpu.VMEM((n_row * SLOT, 128), BF16),
+            pltpu.VMEM((n_row * local_count, 128), BF16),
+            pltpu.VMEM((n * local_count, 128), BF16),
             dma((len(operands) + 3,)),
             dma((2,)),
             dma((2,)),
             dma((8,)),
             dma((8,)),
-            dma((n,)),
-            dma((n,)),
+            dma((n_row,)),
+            dma((n_row,)),
+            dma((n_col,)),
+            dma((n_col,)),
         ],
         compiler_params=pltpu.CompilerParams(
             collective_id=0, has_side_effects=True, vmem_limit_bytes=32 * 1024 * 1024

time: 21.7 us -> 21.8 us (level)
  no operation moved by 1% of the time
where the time goes in v4:
time: 21.8 us; the launch traced here: 21.7 us
  Pallas kernels  21.1 us (97%)
  local copies, waits for them, and re-layouts  0.6 us (3%)
    pallas_call x1, Pallas kernels, on_device(): pl.pallas_call(functools.partial(kernel, (n_row, n_col, ch, rows, cols)),...  21.1 us
    unnamed x1, local copies, waits for them, and re-layouts  0.6 us

profile of v4, /device:TPU:0, one launch (start us, length us, event | category | flops | bytes accessed | tf_op | source)
XLA Modules:
  0.0 21.7 jit_solution(17177338695521140398)
XLA Ops:
  0.0 21.1 %shard_map.118 = bf16[8,256]{1,0:T(8,128)(2,1)S(1)} custom-call(bf16[64,32,128]{2,1,0:T(8,128)(2,1)} %refs_0_.1, bf16[64,576]{1,0:T(8,128)(2,1)} %refs_1_.1, f32[1,64]{1,0:T(1,128)} %bitcast.6, bf16[64,576]{1,0:T(8,128)(2,1)} %refs_3_.1, f32[1,64]{1,0:T(1,128)} %bitcast.7, bf16[4,64]{1,0:T(4,128)(2,1)} %bitcast.5, bf16[256,256]{1,0:T(8,128)(2,1)} %refs_6_.1, ...), custom_call_target="tpu_custom_call" | custom-call | flops 1000000000 | bytes 2000000 | tf_op jit(solution)/shard_map/pallas_call | solution.py:463
  21.1 0.6 %copy.14 = bf16[8,256]{1,0:T(8,128)(2,1)} copy(bf16[8,256]{1,0:T(8,128)(2,1)S(1)} %shard_map.118) | data formatting | bytes 8192

commit v5 on v3

--- a/solution.py
+++ b/solution.py
@@ -189,23 +189,8 @@
         raw[pl.ds(out, 2 * ch), :] = dot(w2a[...], x3[pl.ds(base, 12 * ch), :])
         return carry
 
-    lax.fori_loop(1, half // 2, first_sums, 0)
-
-    pick = iota((owned, embed_ref.shape[0]), 1) == me * owned + iota((owned, embed_ref.shape[0]), 0)
-    own = dot(pick.astype(F32).astype(BF16), embed_ref[...]).astype(BF16)
-    query = dot(own, w_query_ref[...]).astype(BF16).astype(F32)
-    tall = (HEADS * owned, e)
-    own_head = iota(tall, 0) // owned == iota(tall, 1) // HEAD_DIM
-    heads = jnp.where(own_head, jnp.concatenate([query] * HEADS, axis=0), 0.0).astype(BF16)
-    local_count = pos_ref.shape[0]
-    wide = (visible_ref.shape[1], n * local_count)
-    spread = iota(wide, 1) // local_count == iota(wide, 0)
-    blocks = visible_ref.shape
-    mine = iota(blocks, 0) == me * owned // QBLOCK
-    seen_row = jnp.sum(jnp.where(mine, visible_ref[...], 0).astype(F32), axis=0, keepdims=True)
-    seen = dot(
-        jnp.broadcast_to(seen_row, (8, blocks[1])).astype(BF16), spread.astype(F32).astype(BF16)
-    )[0:1] > 0.5
+    for i in range(1, half // 2):
+        first_sums(i, 0)
 
     bias_one = column(bias_one_ref[...])
     bias_two = column(bias_two_ref[...])
@@ -333,15 +318,15 @@
     put(half // 2, 0, *both(half - 1))
     put(half // 2, 1, *joined(inner, rows - 1, outer, 0), blank=(1, r == n_row - 1))
 
-    def second_step(j, acc):
-        base = pl.multiple_of(j * (6 * ch), 6 * ch)
-        return acc + jnp.maximum(dot(w2b[...], f3[pl.ds(base, 12 * ch), :]) + bias_two, 0.0)
-
-    total = lax.fori_loop(0, half // 2, second_step, jnp.zeros((2 * ch, 2 * cols), F32))
+    total = jnp.zeros((2 * ch, 2 * cols), F32)
+    for j in range(half // 2):
+        part = dot(w2b[...], f3[j * (6 * ch) : (j + 2) * (6 * ch), :])
+        total = total + jnp.maximum(part + bias_two, 0.0)
     total = total[:ch] + total[ch:]
     total = total[:, :cols] + total[:, cols:]
     high = total.astype(BF16)
     low = (total - high.astype(F32)).astype(BF16)
+    local_count = pos_ref.shape[0]
     share = SLOT // local_count
     at = iota((SLOT, cols), 0) - local_count * lax.rem(me, share)
     pool = (iota((SLOT, cols), 1) // PATCH == at).astype(F32).astype(BF16)
@@ -373,6 +358,22 @@
         return carry
 
     others(push)
+
+    pick = iota((owned, embed_ref.shape[0]), 1) == me * owned + iota((owned, embed_ref.shape[0]), 0)
+    own = dot(pick.astype(F32).astype(BF16), embed_ref[...]).astype(BF16)
+    query = dot(own, w_query_ref[...]).astype(BF16).astype(F32)
+    tall = (HEADS * owned, e)
+    own_head = iota(tall, 0) // owned == iota(tall, 1) // HEAD_DIM
+    heads = jnp.where(own_head, jnp.concatenate([query] * HEADS, axis=0), 0.0).astype(BF16)
+    wide = (visible_ref.shape[1], n * local_count)
+    spread = iota(wide, 1) // local_count == iota(wide, 0)
+    blocks = visible_ref.shape
+    mine = iota(blocks, 0) == me * owned // QBLOCK
+    seen_row = jnp.sum(jnp.where(mine, visible_ref[...], 0).astype(F32), axis=0, keepdims=True)
+    seen = dot(
+        jnp.broadcast_to(seen_row, (8, blocks[1])).astype(BF16), spread.astype(F32).astype(BF16)
+    )[0:1] > 0.5
+
     others(take)
 
     every = gathered[...].astype(F32).reshape(n // share, share, SLOT, 128).sum(axis=1)

time: 21.7 us -> 20.2 us (0.931)
  Pallas kernels: 20.9 us -> 19.5 us
    pallas_call x1, Pallas kernels: 20.9 us -> 19.5 us  [on_device(): pl.pallas_call(functools.partial(kernel, (n_row, n_col, ch, rows, cols)),...]
where the time goes in v5:
time: 20.2 us; the launch traced here: 20.1 us
  Pallas kernels  19.5 us (97%)
  local copies, waits for them, and re-layouts  0.6 us (3%)
    pallas_call x1, Pallas kernels, on_device(): pl.pallas_call(functools.partial(kernel, (n_row, n_col, ch, rows, cols)),...  19.5 us
    unnamed x1, local copies, waits for them, and re-layouts  0.6 us

profile of v5, /device:TPU:0, one launch (start us, length us, event | category | flops | bytes accessed | tf_op | source)
XLA Modules:
  0.0 20.1 jit_solution(14077982294281275115)
XLA Ops:
  0.0 19.5 %shard_map.118 = bf16[8,256]{1,0:T(8,128)(2,1)S(1)} custom-call(bf16[64,32,128]{2,1,0:T(8,128)(2,1)} %refs_0_.1, bf16[64,576]{1,0:T(8,128)(2,1)} %refs_1_.1, f32[1,64]{1,0:T(1,128)} %bitcast.6, bf16[64,576]{1,0:T(8,128)(2,1)} %refs_3_.1, f32[1,64]{1,0:T(1,128)} %bitcast.7, bf16[4,64]{1,0:T(4,128)(2,1)} %bitcast.5, bf16[256,256]{1,0:T(8,128)(2,1)} %refs_6_.1, ...), custom_call_target="tpu_custom_call" | custom-call | flops 1000000000 | bytes 2000000 | tf_op jit(solution)/shard_map/pallas_call | solution.py:431
  19.5 0.6 %copy.14 = bf16[8,256]{1,0:T(8,128)(2,1)} copy(bf16[8,256]{1,0:T(8,128)(2,1)S(1)} %shard_map.118) | data formatting | bytes 8192

commit v6 on v5

--- a/solution.py
+++ b/solution.py
@@ -293,9 +293,6 @@
             for t, piece in enumerate((left, part, right)):
                 f3[pl.ds(base + (3 * o + t) * ch, ch), where] = piece.astype(BF16)
 
-    def row_of_edge(x, h):
-        return pltpu.roll(x, lax.rem(2 * cols - 4 * h, cols), 1)
-
     def both(h):
         return [(turned(x, -4 * h), turned(x, -4 * (h + 1))) for x in (edge_main, add_main)]
 
@@ -308,19 +305,14 @@
     put(0, 0, *joined(outer, rows - 1, inner, 0), blank=(0, r == 0))
     put(0, 1, *both(half - 1))
 
-    def first_step(i, carry):
-        for side in range(2):
-            h = 2 * i - 1 + side * half
-            put(i, side, *[(row_of_edge(x, h), row_of_edge(x, h + 1)) for x in inner])
-        return carry
-
-    lax.fori_loop(1, half // 2, first_step, 0)
-    put(half // 2, 0, *both(half - 1))
-    put(half // 2, 1, *joined(inner, rows - 1, outer, 0), blank=(1, r == n_row - 1))
-
     total = jnp.zeros((2 * ch, 2 * cols), F32)
-    for j in range(half // 2):
-        part = dot(w2b[...], f3[j * (6 * ch) : (j + 2) * (6 * ch), :])
+    for i in range(1, half // 2 + 1):
+        put(i, 0, *both(2 * i - 1))
+        if i < half // 2:
+            put(i, 1, *both(2 * i - 1 + half))
+        else:
+            put(i, 1, *joined(inner, rows - 1, outer, 0), blank=(1, r == n_row - 1))
+        part = dot(w2b[...], f3[(i - 1) * (6 * ch) : (i + 1) * (6 * ch), :])
         total = total + jnp.maximum(part + bias_two, 0.0)
     total = total[:ch] + total[ch:]
     total = total[:, :cols] + total[:, cols:]

time: 20.2 us -> 19 us (0.941)
  Pallas kernels: 19.5 us -> 18.3 us
    pallas_call x1, Pallas kernels: 19.5 us -> 18.3 us  [on_device(): pl.pallas_call(functools.partial(kernel, (n_row, n_col, ch, rows, cols)),...]
where the time goes in v6:
time: 19 us; the launch traced here: 18.9 us
  Pallas kernels  18.3 us (96%)
  local copies, waits for them, and re-layouts  0.6 us (3%)
    pallas_call x1, Pallas kernels, on_device(): pl.pallas_call(functools.partial(kernel, (n_row, n_col, ch, rows, cols)),...  18.3 us
    unnamed x1, local copies, waits for them, and re-layouts  0.6 us

profile of v6, /device:TPU:0, one launch (start us, length us, event | category | flops | bytes accessed | tf_op | source)
XLA Modules:
  0.0 18.9 jit_solution(6073136667102152884)
XLA Ops:
  0.0 18.3 %shard_map.118 = bf16[8,256]{1,0:T(8,128)(2,1)S(1)} custom-call(bf16[64,32,128]{2,1,0:T(8,128)(2,1)} %refs_0_.1, bf16[64,576]{1,0:T(8,128)(2,1)} %refs_1_.1, f32[1,64]{1,0:T(1,128)} %bitcast.6, bf16[64,576]{1,0:T(8,128)(2,1)} %refs_3_.1, f32[1,64]{1,0:T(1,128)} %bitcast.7, bf16[4,64]{1,0:T(4,128)(2,1)} %bitcast.5, bf16[256,256]{1,0:T(8,128)(2,1)} %refs_6_.1, ...), custom_call_target="tpu_custom_call" | custom-call | flops 1000000000 | bytes 2000000 | tf_op jit(solution)/shard_map/pallas_call | solution.py:423
  18.3 0.6 %copy.14 = bf16[8,256]{1,0:T(8,128)(2,1)} copy(bf16[8,256]{1,0:T(8,128)(2,1)S(1)} %shard_map.118) | data formatting | bytes 8192
